TPU v7x, 256 devices: a whole 4x4x8 slice. The times are simulated.
256 devices in a mesh: dp: 16 (over z, core), expert: 16 (over y, x).
Axes of the slice: x: 4, y: 4, z: 8, core: 2. Of those that a mesh axis runs over, the one named last changes fastest.
Arguments:
- tokens: bfloat16 [32768, 4096], P(('dp', 'expert')), may hold values from -6 to 6
- expert_ids: int32 [32768, 1], P(('dp', 'expert')), may hold values from 0 to 7; in each aligned block of 128 rows (0 to 127, 128 to 255, ...) at most 24 rows name the same one
- gate_values: float32 [32768, 1], P(('dp', 'expert')), may hold values from 0.1 to 1
- cotangent: bfloat16 [32768, 4096], P(('dp', 'expert')), may hold values from -6 to 6
- gate_weight: bfloat16 [4096, 6144], P('dp', 'expert'), may hold values from -0.09375 to 0.09375
- up_weight: bfloat16 [4096, 6144], P('dp', 'expert'), may hold values from -0.09375 to 0.09375
- down_weight: bfloat16 [4096, 6144], P('dp', 'expert'), may hold values from -0.21875 to 0.21875
Outputs:
- moe_out: bfloat16 [32768, 4096], P(('dp', 'expert'))
- token_grad: bfloat16 [32768, 4096], P(('dp', 'expert'))
- gate_grad: float32 [4096, 6144], P('dp', 'expert')
- up_grad: float32 [4096, 6144], P('dp', 'expert')
- down_grad: float32 [4096, 6144], P('dp', 'expert')
Inputs may be any that keep to these rules, and one draw needn't show every extreme that they name: `expert_ids`: within each device's 128 rows no expert is named more than 24 times, and in some of those blocks one expert is named exactly 24 times.
All inputs are finite; a program needn't handle non-finite values.
Results may differ from a plain program's by a relative error of at most 0.02.
Values may be sent and summed in bfloat16 or wider, within the bound.
A program may use at most 128 MiB of HBM per device.

v0:
```python
import jax
import jax.numpy as jnp
from jax import lax
from jax.sharding import PartitionSpec as P


def spread_rows(buffer):
    slot_total, features = buffer.shape
    expert_count = lax.axis_size("expert")
    capacity = slot_total * 2 // expert_count
    outgoing = jnp.broadcast_to(
        buffer.reshape(expert_count // 2, 1, capacity, features),
        (expert_count // 2, 2, capacity, features),
    ).reshape(expert_count, capacity, features)
    received = lax.all_to_all(outgoing, "expert", split_axis=0, concat_axis=0, tiled=True)
    return received.reshape(expert_count * capacity, features)


def return_rows(partial_value):
    row_total, features = partial_value.shape
    expert_count = lax.axis_size("expert")
    capacity = row_total // expert_count
    returned = lax.all_to_all(
        partial_value.reshape(expert_count, capacity, features),
        "expert",
        split_axis=0,
        concat_axis=0,
        tiled=True,
    )
    paired = returned.reshape(expert_count // 2, 2, capacity, features).astype(jnp.float32)
    summed = (paired[:, 0] + paired[:, 1]).astype(jnp.bfloat16)
    return summed.reshape(expert_count // 2 * capacity, features)


def on_device(tokens, expert_ids, gate_values, cotangent, gate_weight, up_weight, down_weight):
    tok_count, features = tokens.shape
    picks = expert_ids.shape[1]
    expert_count = lax.axis_size("expert")
    experts_here = expert_count // 2
    capacity = 3 * tok_count * picks // (2 * experts_here)
    half_units = gate_weight.shape[1]
    full_gate, full_up, full_down = (
        lax.all_gather(gate_weight, "dp", axis=0, tiled=True),
        lax.all_gather(up_weight, "dp", axis=0, tiled=True),
        lax.all_gather(down_weight, "dp", axis=0, tiled=True),
    )
    flat_ids = expert_ids.reshape(-1)
    onehot = (flat_ids[:, None] == jnp.arange(experts_here, dtype=jnp.int32)[None, :]).astype(
        jnp.int32
    )
    before = jnp.cumsum(onehot, axis=0) - onehot
    order = jnp.sum(before * onehot, axis=1)
    position = (flat_ids * capacity + order).reshape(tok_count, picks)
    slot_range = jnp.arange(experts_here * capacity, dtype=jnp.int32)
    select_all = slot_range[:, None, None] == position[None, :, :]
    dispatch = jnp.any(select_all, axis=2).astype(jnp.bfloat16)
    slot_gate = jnp.sum(jnp.where(select_all, gate_values[None, :, :], 0.0), axis=(1, 2))
    expert_local = jnp.dot(dispatch, tokens, preferred_element_type=jnp.float32).astype(
        jnp.bfloat16
    )
    rows_in = spread_rows(expert_local)
    gate_pre = jnp.dot(rows_in, full_gate, preferred_element_type=jnp.float32)
    up_pre = jnp.dot(rows_in, full_up, preferred_element_type=jnp.float32)
    sigmoid_g = jax.nn.sigmoid(gate_pre)
    silu_g = gate_pre * sigmoid_g
    hidden = (silu_g * up_pre).astype(jnp.bfloat16)
    contract_last = (((1,), (1,)), ((), ()))
    partial_value = lax.dot_general(
        hidden, full_down, contract_last, preferred_element_type=jnp.float32
    ).astype(jnp.bfloat16)
    expert_out = return_rows(partial_value)
    pick = 0
    selector = select_all[:, :, pick].T.astype(jnp.bfloat16)
    gathered = jnp.dot(selector, expert_out, preferred_element_type=jnp.float32)
    combined = gate_values * gathered
    moe_out = combined.astype(jnp.bfloat16)
    grad_local = (
        slot_gate[:, None] * jnp.dot(dispatch, cotangent, preferred_element_type=jnp.float32)
    ).astype(jnp.bfloat16)
    grad_rows = spread_rows(grad_local)
    grad_hidden = jnp.dot(grad_rows, full_down, preferred_element_type=jnp.float32)
    grad_gate = (grad_hidden * up_pre * sigmoid_g * (1.0 + gate_pre * (1.0 - sigmoid_g))).astype(
        jnp.bfloat16
    )
    grad_up = (grad_hidden * silu_g).astype(jnp.bfloat16)
    grad_partial = (
        lax.dot_general(grad_gate, full_gate, contract_last, preferred_element_type=jnp.float32)
        + lax.dot_general(grad_up, full_up, contract_last, preferred_element_type=jnp.float32)
    ).astype(jnp.bfloat16)
    grad_in = return_rows(grad_partial)
    pick = 0
    selector = select_all[:, :, pick].T.astype(jnp.bfloat16)
    token_sum = jnp.dot(selector, grad_in, preferred_element_type=jnp.float32)
    token_grad = token_sum.astype(jnp.bfloat16)
    contract_rows = (((0,), (0,)), ((), ()))
    summed = lax.psum_scatter(
        jnp.concatenate(
            [
                lax.dot_general(
                    rows_in, grad_gate, contract_rows, preferred_element_type=jnp.float32
                ),
                lax.dot_general(
                    rows_in, grad_up, contract_rows, preferred_element_type=jnp.float32
                ),
                lax.dot_general(
                    grad_rows, hidden, contract_rows, preferred_element_type=jnp.float32
                ),
            ],
            axis=1,
        ).astype(jnp.bfloat16),
        "dp",
        scatter_dimension=0,
        tiled=True,
    ).astype(jnp.float32)
    gate_grad = summed[:, :half_units]
    up_grad = summed[:, half_units : 2 * half_units]
    down_grad = summed[:, 2 * half_units :]
    return (moe_out, token_grad, gate_grad, up_grad, down_grad)


def solution(mesh):
    return jax.shard_map(
        on_device,
        mesh=mesh,
        in_specs=(
            P(("dp", "expert"), None),
            P(("dp", "expert"), None),
            P(("dp", "expert"), None),
            P(("dp", "expert"), None),
            P("dp", "expert"),
            P("dp", "expert"),
            P("dp", "expert"),
        ),
        out_specs=(
            P(("dp", "expert"), None),
            P(("dp", "expert"), None),
            P("dp", "expert"),
            P("dp", "expert"),
            P("dp", "expert"),
        ),
        check_vma=False,
    )
```

profile of v0, /device:TPU:14, one launch (start us, length us, event | category | flops | bytes accessed | tf_op | source)
XLA Modules:
  0.0 278.5 jit_solution(10820760517413236586)
XLA Ops:
  11.7 2.0 broadcast_in_dim.31
  13.7 7.4 %all-to-all-start = ((bf16[16,24,4096]{2,1,0:T(8,128)(2,1)}), bf16[16,24,4096]{2,1,0:T(8,128)(2,1)S(1)}, u32[]{:S(2)}, u32[]{:S(2)}) async-start(bf16[16,24,4096]{2,1,0:T(8,128)(2,1)} %bitcast.45), calls=%async_computation | async-start | bytes 6291456 | tf_op jit(solution)/shard_map/all_to_all | solution.py:15
  22.0 3.0 %fusion = bf16[192,4096]{1,0:T(8,128)(2,1)} fusion(bf16[128,4096]{1,0:T(8,128)(2,1)} %param.10, f32[192]{0:T(256)S(1)} %select_reduce_fusion, s32[128]{0:T(128)S(1)} %multiply_add_fusion), kind=kOutput, calls=%fused_computation.7 | convolution fusion | flops 202924032 | bytes 2622720 | tf_op jit(solution)/shard_map/dot_general | solution.py:78
  24.9 39.2 %all-to-all-done = bf16[16,24,4096]{2,1,0:T(8,128)(2,1)S(1)} async-done(((bf16[16,24,4096]{2,1,0:T(8,128)(2,1)}), bf16[16,24,4096]{2,1,0:T(8,128)(2,1)S(1)}, u32[]{:S(2)}, u32[]{:S(2)}) %all-to-all-start) | async-done | bytes 3145760 | tf_op jit(solution)/shard_map/all_to_all | solution.py:15
  64.2 3.4 %broadcast_in_dim.35 = bf16[8,2,24,4096]{3,2,1,0:T(8,128)(2,1)} broadcast(bf16[8,24,4096]{2,1,0:T(8,128)(2,1)} %bitcast.50), dimensions={0,2,3} | broadcast | bytes 4718592 | tf_op jit(solution)/shard_map/broadcast_in_dim | solution.py:11
  67.6 8.8 %all-to-all-start.2 = ((bf16[16,24,4096]{2,1,0:T(8,128)(2,1)}), bf16[16,24,4096]{2,1,0:T(8,128)(2,1)}, u32[]{:S(2)}, u32[]{:S(2)}) async-start(bf16[16,24,4096]{2,1,0:T(8,128)(2,1)} %bitcast.46), calls=%async_computation.2 | async-start | bytes 6291456 | tf_op jit(solution)/shard_map/all_to_all | solution.py:15
  76.7 4.5 %fusion.11 = f32[384,384]{1,0:T(8,128)} fusion(bf16[384,4096]{1,0:T(8,128)(2,1)S(1)} %bitcast.39, bf16[4096,384]{1,0:T(8,128)(2,1)} %all-gather.4.cloned.1.call-done), kind=kOutput, calls=%fused_computation.33 | convolution fusion | flops 1207959552 | bytes 6881280 | tf_op jit(solution)/shard_map/dot_general | solution.py:62
  81.2 13.9 %all-gather.6.cloned.1.call-done = bf16[4096,384]{1,0:T(8,128)(2,1)} async-done(((bf16[256,384]{1,0:T(8,128)(2,1)}), bf16[4096,384]{1,0:T(8,128)(2,1)}) %all-gather.6.cloned.1.call-update) | async-done | bytes 3145744 | tf_op jit(solution)/shard_map/all_gather | solution.py:44
  95.1 4.5 %fusion.12 = f32[384,384]{1,0:T(8,128)} fusion(bf16[384,4096]{1,0:T(8,128)(2,1)S(1)} %bitcast.40, bf16[4096,384]{1,0:T(8,128)(2,1)} %all-gather.6.cloned.1.call-done), kind=kOutput, calls=%fused_computation.34 | convolution fusion | flops 1207959552 | bytes 6881280 | tf_op jit(solution)/shard_map/dot_general | solution.py:63
  99.6 17.1 %all-to-all-done.2 = bf16[16,24,4096]{2,1,0:T(8,128)(2,1)} async-done(((bf16[16,24,4096]{2,1,0:T(8,128)(2,1)}), bf16[16,24,4096]{2,1,0:T(8,128)(2,1)}, u32[]{:S(2)}, u32[]{:S(2)}) %all-to-all-start.2) | async-done | bytes 3145760 | tf_op jit(solution)/shard_map/all_to_all | solution.py:15
  116.7 19.6 %all-gather.8.cloned.1.call-done = bf16[4096,384]{1,0:T(8,128)(2,1)} async-done(((bf16[256,384]{1,0:T(8,128)(2,1)}), bf16[4096,384]{1,0:T(8,128)(2,1)}) %all-gather.8.cloned.1.call-update) | async-done | bytes 3145744 | tf_op jit(solution)/shard_map/all_gather | solution.py:45
  136.3 5.0 %multiply_convert_fusion = (bf16[384,384]{1,0:T(8,128)(2,1)S(1)}, bf16[384,384]{1,0:T(8,128)(2,1)S(1)}, bf16[384,384]{1,0:T(8,128)(2,1)S(1)}) fusion(f32[384,384]{1,0:T(8,128)} %fusion.11, f32[384,384]{1,0:T(8,128)} %fusion.12, bf16[384,4096]{1,0:T(8,128)(2,1)} %bitcast.11, bf16[4096,384]{1,0:T(8,128)(2,1)} %all-gather.8.cloned.1.call-done), kind=kOutput, calls=%fused_computation.16 | convolution fusion | flops 1210171392 | bytes 8355840 | tf_op jit(solution)/shard_map/dot_general | solution.py:81
  141.4 3.9 %convolution_convert_fusion = bf16[4096,384]{0,1:T(8,128)(2,1)S(1)} fusion(bf16[384,4096]{1,0:T(8,128)(2,1)} %bitcast.11, bf16[384,384]{1,0:T(8,128)(2,1)S(1)} %get-tuple-element.17), kind=kOutput, calls=%fused_computation.2 | convolution fusion | flops 1209532416 | bytes 6586368 | tf_op jit(solution)/shard_map/dot_general | solution.py:105
  145.3 1.8 convolution_convert_fusion.1
  147.2 1.8 convolution_convert_fusion.2
  149.0 4.3 %pad_maximum_fusion = bf16[4096,1152]{0,1:T(8,128)(2,1)} fusion(bf16[4096,384]{0,1:T(8,128)(2,1)S(1)} %convolution_convert_fusion, bf16[4096,384]{0,1:T(8,128)(2,1)S(1)} %convolution_convert_fusion.1, bf16[4096,384]{0,1:T(8,128)(2,1)S(1)} %convolution_convert_fusion.2), kind=kLoop, calls=%fused_computation | loop fusion | flops 28311552 | bytes 18874368 | tf_op jit(solution)/shard_map/concatenate | solution.py:97
  153.3 0.9 copy-done.5
  154.3 5.4 %convolution_convert_fusion.3 = bf16[384,4096]{1,0:T(8,128)(2,1)} fusion(bf16[384,384]{1,0:T(8,128)(2,1)S(1)} %copy-done.5, bf16[4096,384]{1,0:T(8,128)(2,1)} %all-gather.8.cloned.1.call-done), kind=kOutput, calls=%fused_computation.5 | convolution fusion | flops 1209532416 | bytes 6586368 | tf_op jit(solution)/shard_map/dot_general | solution.py:68
  159.7 7.2 %all-to-all-start.1 = ((bf16[16,24,4096]{2,1,0:T(8,128)(2,1)}), bf16[16,24,4096]{2,1,0:T(8,128)(2,1)S(1)}, u32[]{:S(2)}, u32[]{:S(2)}) async-start(bf16[16,24,4096]{2,1,0:T(8,128)(2,1)} %bitcast.53), calls=%async_computation.1 | async-start | bytes 6291456 | tf_op jit(solution)/shard_map/all_to_all | solution.py:23
  166.9 3.9 %fusion.13 = f32[384,4096]{1,0:T(8,128)S(1)} fusion(bf16[384,384]{1,0:T(8,128)(2,1)} %copy-done.3, bf16[4096,384]{1,0:T(8,128)(2,1)} %all-gather.4.cloned.1.call-done), kind=kOutput, calls=%fused_computation.35 | convolution fusion | flops 1207959552 | bytes 9732096 | tf_op jit(solution)/shard_map/dot_general | solution.py:87
  170.9 3.6 %add_convert_fusion = bf16[384,4096]{1,0:T(8,128)(2,1)} fusion(f32[384,4096]{1,0:T(8,128)S(1)} %fusion.13, bf16[384,384]{1,0:T(8,128)(2,1)S(1)} %get-tuple-element.15, bf16[4096,384]{1,0:T(8,128)(2,1)S(1)} %copy-done.2), kind=kOutput, calls=%fused_computation.1 | convolution fusion | flops 1211105280 | bytes 12877824 | tf_op jit(solution)/shard_map/dot_general | solution.py:88
  174.5 37.6 %all-to-all-done.1 = bf16[16,24,4096]{2,1,0:T(8,128)(2,1)S(1)} async-done(((bf16[16,24,4096]{2,1,0:T(8,128)(2,1)}), bf16[16,24,4096]{2,1,0:T(8,128)(2,1)S(1)}, u32[]{:S(2)}, u32[]{:S(2)}) %all-to-all-start.1) | async-done | bytes 3145760 | tf_op jit(solution)/shard_map/all_to_all | solution.py:23
  212.1 7.9 %all-to-all-start.3 = ((bf16[16,24,4096]{2,1,0:T(8,128)(2,1)}), bf16[16,24,4096]{2,1,0:T(8,128)(2,1)}, u32[]{:S(2)}, u32[]{:S(2)}) async-start(bf16[16,24,4096]{2,1,0:T(8,128)(2,1)} %bitcast.48), calls=%async_computation.3 | async-start | bytes 6291456 | tf_op jit(solution)/shard_map/all_to_all | solution.py:23
  220.0 3.4 %convert.14 = f32[8,2,24,4096]{3,2,1,0:T(8,128)} convert(bf16[8,2,24,4096]{3,2,1,0:T(8,128)(2,1)S(1)} %bitcast.47) | non-fusion elementwise | flops 1572864 | bytes 9437184 | tf_op jit(solution)/shard_map/convert_element_type | solution.py:30
  223.4 38.1 %all-to-all-done.3 = bf16[16,24,4096]{2,1,0:T(8,128)(2,1)} async-done(((bf16[16,24,4096]{2,1,0:T(8,128)(2,1)}), bf16[16,24,4096]{2,1,0:T(8,128)(2,1)}, u32[]{:S(2)}, u32[]{:S(2)}) %all-to-all-start.3) | async-done | bytes 3145760 | tf_op jit(solution)/shard_map/all_to_all | solution.py:23
  261.5 2.8 %convert.15 = f32[8,2,24,4096]{3,2,1,0:T(8,128)S(1)} convert(bf16[8,2,24,4096]{3,2,1,0:T(8,128)(2,1)} %bitcast.14) | non-fusion elementwise | flops 1572864 | bytes 9437184 | tf_op jit(solution)/shard_map/convert_element_type | solution.py:30
  264.7 1.5 convolution_convert_fusion.5
  266.6 1.5 fusion.1
  268.0 1.2 fusion.10
  269.2 0.9 copy.15
  270.2 0.9 copy.16
  271.1 0.9 copy.17
  (36 shorter events, 6.3 us)
Async XLA Ops:
  7.2 3.9 %copy-start = (bf16[128,4096]{1,0:T(8,128)(2,1)S(1)}, bf16[128,4096]{1,0:T(8,128)(2,1)}, u32[]{:S(2)}) copy-start(bf16[128,4096]{1,0:T(8,128)(2,1)} %param.7) | copy-start | bytes 3145732
  7.2 69.5 %all-gather.4.cloned.1.call-start = ((), (), s32[]{:S(2)}) async-start(), calls=%async_computation.5 | async-start | bytes 3342336 | tf_op jit(solution)/shard_map/all_gather | solution.py:43
  7.9 87.2 %all-gather.6.cloned.1.call-start = ((), (), s32[]{:S(2)}) async-start(), calls=%async_computation.6 | async-start | bytes 3342336 | tf_op jit(solution)/shard_map/all_gather | solution.py:44
  13.7 8.2 %copy-start.6 = (f32[128,1]{0,1:T(1,128)S(1)}, f32[128,1]{0,1:T(1,128)}, u32[]{:S(2)}) copy-start(f32[128,1]{0,1:T(1,128)} %param.9) | copy-start | bytes 1540
  13.7 50.5 %all-to-all-start = ((bf16[16,24,4096]{2,1,0:T(8,128)(2,1)}), bf16[16,24,4096]{2,1,0:T(8,128)(2,1)S(1)}, u32[]{:S(2)}, u32[]{:S(2)}) async-start(bf16[16,24,4096]{2,1,0:T(8,128)(2,1)} %bitcast.45), calls=%async_computation | async-start | bytes 6291456 | tf_op jit(solution)/shard_map/all_to_all | solution.py:15
  21.1 115.2 %all-gather.8.cloned.1.call-start = ((), (), s32[]{:S(2)}) async-start(), calls=%async_computation.7 | async-start | bytes 3342336 | tf_op jit(solution)/shard_map/all_gather | solution.py:45
  67.6 49.1 %all-to-all-start.2 = ((bf16[16,24,4096]{2,1,0:T(8,128)(2,1)}), bf16[16,24,4096]{2,1,0:T(8,128)(2,1)}, u32[]{:S(2)}, u32[]{:S(2)}) async-start(bf16[16,24,4096]{2,1,0:T(8,128)(2,1)} %bitcast.46), calls=%async_computation.2 | async-start | bytes 6291456 | tf_op jit(solution)/shard_map/all_to_all | solution.py:15
  76.4 191.6 %reduce-scatter.2.cloned.1.call-start = ((), (), s32[]{:S(2)}) async-start(), calls=%async_computation.8 | async-start | bytes 10027008 | tf_op jit(solution)/shard_map/reduce_scatter | solution.py:96
  141.3 4.0 %copy-start.4 = (bf16[384,384]{1,0:T(8,128)(2,1)}, bf16[384,384]{1,0:T(8,128)(2,1)S(1)}, u32[]{:S(2)}) copy-start(bf16[384,384]{1,0:T(8,128)(2,1)S(1)} %get-tuple-element.17) | copy-start | bytes 884740
  141.3 5.8 %copy-start.3 = (bf16[384,384]{1,0:T(8,128)(2,1)}, bf16[384,384]{1,0:T(8,128)(2,1)S(1)}, u32[]{:S(2)}) copy-start(bf16[384,384]{1,0:T(8,128)(2,1)S(1)} %get-tuple-element.16) | copy-start | bytes 884740
  153.3 1.0 copy-start.5
  159.7 52.4 %all-to-all-start.1 = ((bf16[16,24,4096]{2,1,0:T(8,128)(2,1)}), bf16[16,24,4096]{2,1,0:T(8,128)(2,1)S(1)}, u32[]{:S(2)}, u32[]{:S(2)}) async-start(bf16[16,24,4096]{2,1,0:T(8,128)(2,1)} %bitcast.53), calls=%async_computation.1 | async-start | bytes 6291456 | tf_op jit(solution)/shard_map/all_to_all | solution.py:23
  166.9 4.0 %copy-start.2 = (bf16[4096,384]{1,0:T(8,128)(2,1)S(1)}, bf16[4096,384]{1,0:T(8,128)(2,1)}, u32[]{:S(2)}) copy-start(bf16[4096,384]{1,0:T(8,128)(2,1)} %all-gather.6.cloned.1.call-done) | copy-start | bytes 9437188
  212.1 49.5 %all-to-all-start.3 = ((bf16[16,24,4096]{2,1,0:T(8,128)(2,1)}), bf16[16,24,4096]{2,1,0:T(8,128)(2,1)}, u32[]{:S(2)}, u32[]{:S(2)}) async-start(bf16[16,24,4096]{2,1,0:T(8,128)(2,1)} %bitcast.48), calls=%async_computation.3 | async-start | bytes 6291456 | tf_op jit(solution)/shard_map/all_to_all | solution.py:23
  261.5 4.6 %slice-start = ((s8[6291456]{0:T(1024)(128)(4,1)}), s8[4194304]{0:T(1024)(128)(4,1)S(1)}, s32[]{:S(2)}) async-start(s8[6291456]{0:T(1024)(128)(4,1)} %bitcast.43), calls=%async_computation.9 | async-start | bytes 8388608
  264.3 1.8 slice-start.1
  266.5 5.4 %copy-start.1 = (bf16[128,4096]{1,0:T(8,128)(2,1)S(1)}, bf16[128,4096]{1,0:T(8,128)(2,1)}, u32[]{:S(2)}) copy-start(bf16[128,4096]{1,0:T(8,128)(2,1)} %param.7) | copy-start | bytes 3145732
Sparse Core Ops, SparseCore 0:
  9.8 43.8 all-gather.3
  55.6 39.4 all-gather.5
  97.0 39.2 all-gather.7
  153.5 72.7 reduce-scatter.1
where the time goes:
time: 284 us; the launch traced here: 279 us
  waiting for transfers between devices  168 us (59%)
  matrix products  41 us (14%)
  starting transfers between devices  31.8 us (11%)
  between operations  13.9 us (5%)
  other arithmetic  13.8 us (5%)
  local copies, waits for them, and re-layouts  10.4 us (4%)
    all_to_all x2, waiting for transfers between devices, return_rows(): lax.all_to_all(partial_value.reshape(expert_count, capacity, features), '...  75.7 us
    all_to_all x2, waiting for transfers between devices, spread_rows(): lax.all_to_all(outgoing, 'expert', split_axis=0, concat_axis=0, tiled=True)  56.3 us
    all_gather x1, waiting for transfers between devices, on_device(): lax.all_gather(down_weight, 'dp', axis=0, tiled=True)  19.6 us
    all_to_all x2, starting transfers between devices, spread_rows(): lax.all_to_all(outgoing, 'expert', split_axis=0, concat_axis=0, tiled=True)  16.3 us
    all_to_all x2, starting transfers between devices, return_rows(): lax.all_to_all(partial_value.reshape(expert_count, capacity, features), '...  15.2 us
    all_gather x1, waiting for transfers between devices, on_device(): lax.all_gather(up_weight, 'dp', axis=0, tiled=True)  13.9 us
    convert_element_type x2, other arithmetic, return_rows(): returned.reshape(expert_count // 2, 2, capacity, features)  6.24 us
  transfers between devices with their start and end apart: 8, of which 6 were waited for; matrix products, arithmetic and copies ran while one was open for 16% of the time, Pallas kernels for 0%

commit v1 on v0

v1 whole, which is shorter than its diff:
```python
import functools

import jax
import jax.numpy as jnp
from jax import lax
from jax.experimental import pallas as pl
from jax.experimental.pallas import tpu as pltpu
from jax.sharding import PartitionSpec as P

MESH = pl.DeviceIdType.MESH
BF, F32 = jnp.bfloat16, jnp.float32
HOPS = ({1: 4, -1: 3}, {1: 3, -1: 4}, {1: 4, -1: 3})
TOK, OUT = 0, 0
COT, GRAD = 1, 1
OWN, PAR, NBR, FWD = 0, 1, 2, 3
CAP = 24
SLAB = 2 * CAP
BLK = 256
N_SEM = 190


def kernel(
    tok, ids, gv, cot, wg, wu, wd,
    o_moe, o_tok, o_gate, o_up, o_down,
    w_all, s_buf, own_buf, oth_buf, par_buf, nbr_buf, fwd_buf, x_buf, part, back_own, back_nbr,
    back_oth, res, sib_buf, ring_buf, pre, act, sel, ssem, rsem, lsem,
):
    nz = w_all.shape[1]
    units = wg.shape[1]
    half = s_buf.shape[-1]
    rows = x_buf.shape[1]
    tiles = half // BLK
    dp, ex = lax.axis_index("dp"), lax.axis_index("expert")
    z, c = lax.div(dp, 2), lax.rem(dp, 2)
    y, x = lax.div(ex, 4), lax.rem(ex, 4)
    p = lax.div(x, 2)
    partner = (dp, ex + 1 - 2 * lax.rem(x, 2))
    neighbour = (dp, y * 4 + 3 - x)
    sibling = (dp + 1 - 2 * c, ex)

    def zdev(d):
        return (lax.rem(z + nz + d, nz) * 2 + c, ex)

    def ydev(r):
        return (dp, lax.rem(y + r, 4) * 4 + x)

    def expert_at(r, other):
        mine = lax.rem(y + r, 4) * 2 + p
        return mine + (1 - 2 * p) if other else mine

    barrier = pltpu.get_barrier_semaphore()
    for dev in (partner, neighbour, sibling, zdev(1), zdev(-1), ydev(1), ydev(2), ydev(3)):
        pl.semaphore_signal(barrier, inc=1, device_id=dev, device_id_type=MESH)
    pl.semaphore_wait(barrier, 8)

    copies, received, sent = {}, set(), set()

    def send(key, src, dst, dev):
        i = len(copies)
        copy = pltpu.make_async_remote_copy(
            src_ref=src, dst_ref=dst, send_sem=ssem.at[i], recv_sem=rsem.at[i],
            device_id=dev, device_id_type=MESH,
        )
        copy.start()
        copies[key] = copy

    def got(*key):
        if key not in received:
            received.add(key)
            copies[key].wait_recv()

    def drain(*kinds):
        for key, copy in copies.items():
            if key not in sent and (not kinds or key[0] in kinds):
                sent.add(key)
                copy.wait_send()

    shards = (wg, wu, wd)

    def cols(m):
        return slice(m * units, (m + 1) * units)

    def zpos(off):
        return lax.rem(z + nz + off, nz)

    def w_start(m):
        for d in (1, -1):
            send(("w", m, d, 1), shards[m], w_all.at[c, z, :, cols(m)], zdev(d))

    def w_arrive(m, s):
        for d in (1, -1):
            if s <= HOPS[m][d]:
                got("w", m, d, s)
                block = w_all.at[c, zpos(-d * s), :, cols(m)]
                if s < HOPS[m][d]:
                    send(("w", m, d, s + 1), block, block, zdev(d))
                send(("ws", m, d, s), block, block, sibling)

    def w_ready(m):
        for d in (1, -1):
            for s in range(1, HOPS[m][d] + 1):
                got("w", m, d, s)
                got("ws", m, d, s)
        got("ws", m, 0, 0)

    w_start(0)
    w_start(1)
    local = []
    for m in range(3):
        send(("ws", m, 0, 0), shards[m], w_all.at[c, z, :, cols(m)], sibling)
        local.append(pltpu.make_async_copy(shards[m], w_all.at[c, z, :, cols(m)], lsem.at[m]))
        local[-1].start()

    ntok = ids.shape[0]
    idv = ids[...]
    lane = lax.broadcasted_iota(jnp.int32, (ntok, 128), 1)
    onehot = jnp.where(idv == lane, 1.0, 0.0).astype(F32)
    lower = jnp.where(
        lax.broadcasted_iota(jnp.int32, (ntok, ntok), 0)
        > lax.broadcasted_iota(jnp.int32, (ntok, ntok), 1), 1.0, 0.0,
    ).astype(BF)
    before = jnp.dot(lower, onehot.astype(BF), preferred_element_type=F32)
    order = jnp.sum(before * onehot, axis=1, keepdims=True).astype(jnp.int32)
    place = idv * SLAB + order
    slot = lax.broadcasted_iota(jnp.int32, (ntok, sel.shape[2]), 1)
    for h in range(2):
        sel[h] = jnp.where(slot == place + h * CAP, 1.0, 0.0).astype(BF)

    def dispatch(ph, source):
        def body(j, carry):
            acc = None
            for h in range(2):
                at = pl.ds(pl.multiple_of(h * half + j * BLK, BLK), BLK)
                term = lax.dot_general(
                    sel[h], source(at), (((0,), (0,)), ((), ())), preferred_element_type=F32
                )
                acc = term if acc is None else acc + term
            at = pl.ds(pl.multiple_of(j * BLK, BLK), BLK)
            s_buf[ph, :, :, at] = acc.astype(BF).reshape(8, SLAB, BLK)
            return carry

        lax.fori_loop(0, tiles, body, 0)

    def y_sends(ph):
        for r in (1, 3):
            send(("own", ph, r), s_buf.at[ph, expert_at(r, False)], own_buf.at[ph, r - 1], ydev(r))
        for r in (1, 3):
            send(("oth", ph, r), s_buf.at[ph, expert_at(r, True)], oth_buf.at[ph, r - 1], ydev(r))
        send(("own", ph, 2), s_buf.at[ph, expert_at(2, False)], own_buf.at[ph, 1], ydev(2))
        send(("oth", ph, 2), s_buf.at[ph, expert_at(2, True)], oth_buf.at[ph, 1], ydev(2))

    def self_par(ph):
        send(("par", ph, 0), s_buf.at[ph, expert_at(0, False)], par_buf.at[ph, 0], partner)

    def self_nbr(ph):
        send(("nbr", ph, 0), s_buf.at[ph, expert_at(0, True)], nbr_buf.at[ph, 0], neighbour)

    def t_own(ph, r):
        got("own", ph, r)
        send(("par", ph, r), own_buf.at[ph, r - 1], par_buf.at[ph, r], partner)

    def t_oth(ph, r):
        got("oth", ph, r)
        send(("nbr", ph, r), oth_buf.at[ph, r - 1], nbr_buf.at[ph, r], neighbour)

    def t_nbr(ph, r):
        got("nbr", ph, r)
        send(("fwd", ph, r), nbr_buf.at[ph, r], fwd_buf.at[ph, r], partner)

    wide = 512

    def gather_rows(ph):
        for r in range(4):
            got("par", ph, r)
            got("fwd", ph, r)

        def slab(g, r, at):
            if g == OWN:
                if r == 0:
                    return s_buf[ph, expert_at(0, False), :, at]
                return own_buf[ph, r - 1, :, at]
            return {PAR: par_buf, NBR: nbr_buf, FWD: fwd_buf}[g][ph, r, :, at]

        def body(j, carry):
            at = pl.ds(pl.multiple_of(j * wide, wide), wide)
            for g in range(4):
                for r in (0, 2):
                    first = slab(g, r, at).astype(F32)
                    second = slab(g, r + 1, at).astype(F32)
                    base = (g * 4 + r) * CAP
                    for h in range(2):
                        both = jnp.concatenate(
                            [first[h * CAP:(h + 1) * CAP], second[h * CAP:(h + 1) * CAP]], axis=0
                        )
                        to = pl.ds(pl.multiple_of(h * half + j * wide, wide), wide)
                        x_buf[ph, base:base + SLAB, to] = both.astype(BF)
            return carry

        lax.fori_loop(0, half // wide, body, 0)

    def project(ph, m, width):
        pre_at = slice(0, width)

        def body(j, carry):
            acc = None
            for k in range(2):
                at = pl.ds(pl.multiple_of(j * 2 * BLK + k * BLK, BLK), BLK)
                term = jnp.dot(
                    x_buf[ph, :, at], w_all[k, j, :, m * units:m * units + width],
                    preferred_element_type=F32,
                )
                acc = term if acc is None else acc + term
            pre_to[:, pre_at] += acc
            return carry

        pre_to = pre if ph == TOK else grad_hidden
        pre_to[:, pre_at] = jnp.zeros((rows, width), F32)
        lax.fori_loop(0, nz, body, 0)

    grad_hidden = pre.at[:, 2 * units:3 * units]
    tall = 32

    def activate():
        def body(i, carry):
            at = pl.ds(pl.multiple_of(i * tall, tall), tall)
            gate, up = pre[at, cols(0)], pre[at, cols(1)]
            act[at, cols(2)] = (gate * jax.nn.sigmoid(gate) * up).astype(BF)
            return carry

        lax.fori_loop(0, rows // tall, body, 0)

    def differentiate():
        def body(i, carry):
            at = pl.ds(pl.multiple_of(i * tall, tall), tall)
            gate, up, grad = pre[at, cols(0)], pre[at, cols(1)], pre[at, cols(2)]
            sig = jax.nn.sigmoid(gate)
            act[at, cols(0)] = (grad * up * sig * (1.0 + gate * (1.0 - sig))).astype(BF)
            act[at, cols(1)] = (grad * (gate * sig)).astype(BF)
            return carry

        lax.fori_loop(0, rows // tall, body, 0)

    def partials(ph, at_units):
        def body(j, carry):
            k, zz = lax.rem(j, 2), lax.div(j, 2)
            both = []
            for h in range(2):
                value = lax.dot_general(
                    act[:, at_units], w_all[k, zz + h * (nz // 2), :, at_units],
                    (((1,), (1,)), ((), ())), preferred_element_type=F32,
                )
                both.append(value.reshape(rows // CAP, CAP, BLK))
            joined = jnp.concatenate(both, axis=1).astype(BF).reshape(4, 4, SLAB, BLK)
            part[ph, :, :, :, pl.ds(pl.multiple_of(j * BLK, BLK), BLK)] = joined
            return carry

        lax.fori_loop(0, tiles, body, 0)

    def pair_sends(ph):
        for r in range(4):
            send(("bn", ph, r), part.at[ph, FWD, r], back_nbr.at[ph, r], partner)
        for r in range(4):
            send(("bo", ph, r), part.at[ph, PAR, r], back_own.at[ph, r], partner)

    def add_into(dst, a, b):
        def body(j, carry):
            at = pl.ds(pl.multiple_of(j * wide, wide), wide)
            dst[:, at] = (a[:, at].astype(F32) + b[:, at].astype(F32)).astype(BF)
            return carry

        lax.fori_loop(0, half // wide, body, 0)

    def back_n(ph, r):
        got("bn", ph, r)
        mine = part.at[ph, NBR, r]
        add_into(mine, mine, back_nbr.at[ph, r])
        send(("bx", ph, r), mine, back_oth.at[ph, r], neighbour)

    def back_o(ph, r):
        got("bo", ph, r)
        mine = part.at[ph, OWN, r]
        e = expert_at(0, False)
        if r == 0:
            add_into(res.at[ph, e], mine, back_own.at[ph, r])
        else:
            add_into(mine, mine, back_own.at[ph, r])
            send(("ro", ph, r), mine, res.at[ph, e], ydev(4 - r))

    def back_x(ph, r):
        got("bx", ph, r)
        e = expert_at(0, True)
        if r == 0:
            res[ph, e] = back_oth[ph, 0]
        else:
            send(("rx", ph, r), back_oth.at[ph, r], res.at[ph, e], ydev(4 - r))

    def combine(ph, out, scale):
        for r in (1, 2, 3):
            got("ro", ph, r)
            got("rx", ph, r)

        def body(j, carry):
            at = pl.ds(pl.multiple_of(j * BLK, BLK), BLK)
            rows_back = res[ph, :, :, at].reshape(8 * SLAB, BLK)
            for h in range(2):
                value = jnp.dot(sel[h], rows_back, preferred_element_type=F32)
                if scale:
                    value = value * gv[...]
                out[:, pl.ds(pl.multiple_of(h * half + j * BLK, BLK), BLK)] = value.astype(BF)
            return carry

        lax.fori_loop(0, tiles, body, 0)

    def offset(j):
        odd = lax.rem(j, 2)
        return 4 + lax.div(j, 2) * (1 - odd) - lax.div(j + 1, 2) * odd

    def weight_block(k, zz):
        at = pl.ds(pl.multiple_of((zz * 2 + k) * BLK, BLK), BLK)
        by_rows = (((0,), (0,)), ((), ()))
        w_all[k, zz, :, 0:2 * units] = lax.dot_general(
            x_buf[TOK, :, at], act[:, 0:2 * units], by_rows, preferred_element_type=F32
        ).astype(BF)
        w_all[k, zz, :, cols(2)] = lax.dot_general(
            x_buf[COT, :, at], act[:, cols(2)], by_rows, preferred_element_type=F32
        ).astype(BF)

    def weight_grads(k, to_sibling):
        base = len(copies)

        def piece(j, off):
            return pltpu.make_async_remote_copy(
                src_ref=w_all.at[k, zpos(off)], dst_ref=sib_buf.at[off], send_sem=ssem.at[base + j],
                recv_sem=rsem.at[base + j], device_id=sibling, device_id_type=MESH,
            )

        def body(j, carry):
            off = offset(j)
            weight_block(k, zpos(off))
            if to_sibling:
                piece(j, off).start()
            return carry

        lax.fori_loop(0, nz, body, 0)
        if to_sibling:
            for j, off in enumerate((4, 3, 5, 2, 6, 1, 7, 0)):
                copies["sib", off] = piece(j, off)

    ring_slots = {}

    def slot_of(*key):
        return ring_buf.at[ring_slots.setdefault(key, len(ring_slots))]

    def ring_send(m, s):
        for d in (1, -1):
            hops = HOPS[m][d]
            if s < hops:
                off = (d * (hops - s)) % nz
                got("sib", off)
                block = w_all.at[c, zpos(off), :, cols(m)]
                total = block[...].astype(F32) + sib_buf[off, :, cols(m)].astype(F32)
                if s > 0:
                    got("ring", m, d, s - 1)
                    total = total + slot_of(m, d, s - 1)[...].astype(F32)
                block[...] = total.astype(BF)
                send(("ring", m, d, s), block, slot_of(m, d, s), zdev(d))

    def ring_end(m, out):
        got("sib", 0)
        total = w_all[c, z, :, cols(m)].astype(F32) + sib_buf[0, :, cols(m)].astype(F32)
        for d in (1, -1):
            last = HOPS[m][d] - 1
            got("ring", m, d, last)
            total = total + slot_of(m, d, last)[...].astype(F32)
        out[...] = total

    dispatch(TOK, lambda at: tok[:, at])
    self_par(TOK)
    self_nbr(TOK)
    y_sends(TOK)
    dispatch(COT, lambda at: (gv[...] * cot[:, at].astype(F32)).astype(BF))
    w_arrive(0, 1)
    t_own(TOK, 1)
    t_own(TOK, 3)
    t_nbr(TOK, 0)
    w_arrive(1, 1)
    t_oth(TOK, 1)
    t_oth(TOK, 3)
    w_arrive(0, 2)
    t_own(TOK, 2)
    t_nbr(TOK, 1)
    t_oth(TOK, 2)
    w_arrive(1, 2)
    t_nbr(TOK, 3)
    y_sends(COT)
    self_nbr(COT)
    w_arrive(0, 3)
    t_nbr(TOK, 2)
    w_arrive(1, 3)
    self_par(COT)
    w_start(2)
    t_own(COT, 1)
    t_own(COT, 3)
    t_oth(COT, 1)
    t_oth(COT, 3)
    w_arrive(0, 4)
    w_arrive(1, 4)
    t_own(COT, 2)
    t_oth(COT, 2)
    t_nbr(COT, 0)
    gather_rows(TOK)
    w_arrive(2, 1)
    t_nbr(COT, 1)
    for copy in local:
        copy.wait()
    w_ready(0)
    w_ready(1)
    project(TOK, 0, 2 * units)
    w_arrive(2, 2)
    t_nbr(COT, 3)
    t_nbr(COT, 2)
    activate()
    w_arrive(2, 3)
    w_arrive(2, 4)
    w_ready(2)
    partials(OUT, cols(2))
    gather_rows(COT)
    pair_sends(OUT)
    project(COT, 2, units)
    differentiate()
    partials(GRAD, slice(0, 2 * units))
    pair_sends(GRAD)
    drain("w", "ws")
    weight_grads(1 - c, True)
    weight_grads(c, False)
    for m in range(3):
        ring_send(m, 0)
    back_n(OUT, 0)
    back_n(OUT, 1)
    for m in range(3):
        ring_send(m, 1)
    back_n(OUT, 2)
    back_x(OUT, 0)
    back_x(OUT, 1)
    back_n(OUT, 3)
    back_x(OUT, 2)
    back_o(OUT, 1)
    back_o(OUT, 2)
    for m in range(3):
        ring_send(m, 2)
    back_x(OUT, 3)
    back_o(OUT, 3)
    back_o(OUT, 0)
    back_n(GRAD, 0)
    back_n(GRAD, 1)
    for m in range(3):
        ring_send(m, 3)
    combine(OUT, o_moe, True)
    back_n(GRAD, 2)
    back_x(GRAD, 0)
    back_x(GRAD, 1)
    back_n(GRAD, 3)
    back_x(GRAD, 2)
    back_o(GRAD, 1)
    back_x(GRAD, 3)
    back_o(GRAD, 2)
    back_o(GRAD, 3)
    back_o(GRAD, 0)
    for m, out in enumerate((o_gate, o_up, o_down)):
        ring_end(m, out)
    combine(GRAD, o_tok, False)
    drain()


def on_device(tokens, expert_ids, gate_values, cotangent, gate_weight, up_weight, down_weight):
    ntok, features = tokens.shape
    depth, units = gate_weight.shape
    nz = lax.axis_size("dp") // 2
    half = features // 2
    rows = 16 * CAP
    slab = (SLAB, half)
    return pl.pallas_call(
        kernel,
        out_shape=(
            jax.ShapeDtypeStruct((ntok, features), BF),
            jax.ShapeDtypeStruct((ntok, features), BF),
            jax.ShapeDtypeStruct((depth, units), F32),
            jax.ShapeDtypeStruct((depth, units), F32),
            jax.ShapeDtypeStruct((depth, units), F32),
        ),
        in_specs=[pl.BlockSpec(memory_space=pltpu.VMEM)] * 7,
        out_specs=(pl.BlockSpec(memory_space=pltpu.VMEM),) * 5,
        scratch_shapes=[
            pltpu.VMEM((2, nz, depth, 3 * units), BF),
            pltpu.VMEM((2, 8) + slab, BF),
            pltpu.VMEM((2, 3) + slab, BF),
            pltpu.VMEM((2, 3) + slab, BF),
            pltpu.VMEM((2, 4) + slab, BF),
            pltpu.VMEM((2, 4) + slab, BF),
            pltpu.VMEM((2, 4) + slab, BF),
            pltpu.VMEM((2, rows, features), BF),
            pltpu.VMEM((2, 4, 4) + slab, BF),
            pltpu.VMEM((2, 4) + slab, BF),
            pltpu.VMEM((2, 4) + slab, BF),
            pltpu.VMEM((2, 4) + slab, BF),
            pltpu.VMEM((2, 8) + slab, BF),
            pltpu.VMEM((nz, depth, 3 * units), BF),
            pltpu.VMEM((21, depth, units), BF),
            pltpu.VMEM((rows, 3 * units), F32),
            pltpu.VMEM((rows, 3 * units), BF),
            pltpu.VMEM((2, ntok, 8 * SLAB), BF),
            pltpu.SemaphoreType.DMA((N_SEM,)),
            pltpu.SemaphoreType.DMA((N_SEM,)),
            pltpu.SemaphoreType.DMA((3,)),
        ],
        compiler_params=pltpu.CompilerParams(
            collective_id=0, has_side_effects=True, vmem_limit_bytes=62 * 1024 * 1024
        ),
        cost_estimate=pl.CostEstimate(
            flops=18 * rows * features * units, bytes_accessed=8 * ntok * features,
            transcendentals=2 * rows * units,
        ),
    )(tokens, expert_ids, gate_values, cotangent, gate_weight, up_weight, down_weight)


def solution(mesh):
    rows, weights = P(("dp", "expert"), None), P("dp", "expert")
    return jax.shard_map(
        on_device,
        mesh=mesh,
        in_specs=(rows, rows, rows, rows, weights, weights, weights),
        out_specs=(rows, rows, weights, weights, weights),
        check_vma=False,
    )
```

time: 284 us -> 177 us (0.62)
  waiting for transfers between devices: 168 us -> 0 us
  Pallas kernels: 0 us -> 165 us
  matrix products: 41 us -> 0 us
  starting transfers between devices: 31.8 us -> 0 us
  other arithmetic: 13.8 us -> 0 us
  between operations: 13.9 us -> 0.66 us
    pallas_call x0 -> x1, Pallas kernels: none -> 165 us  [on_device(): pl.pallas_call(kernel, out_shape=(jax.ShapeDtypeStruct((ntok, features),...]
    all_to_all x4 -> x0, waiting for transfers between devices: 132 us -> none  [the longest x2 75.7 us: return_rows(): lax.all_to_all(partial_value.reshape(expert_count, capacity, features), '...]
    dot_general x13 -> x0, matrix products: 41 us -> none  [the longest x1 5.4 us: on_device(): lax.dot_general(hidden, full_down, contract_last, preferred_element_type=...]
    all_gather x3 -> x0, waiting for transfers between devices: 33.5 us -> none  [the longest x1 19.6 us: on_device(): lax.all_gather(down_weight, 'dp', axis=0, tiled=True)]
    all_to_all x4 -> x0, starting transfers between devices: 31.4 us -> none  [the longest x2 16.3 us: spread_rows(): lax.all_to_all(outgoing, 'expert', split_axis=0, concat_axis=0, tiled=True)]
    convert_element_type x5 -> x0, other arithmetic: 7.68 us -> none  [the longest x2 6.24 us: return_rows(): returned.reshape(expert_count // 2, 2, capacity, features)]
    broadcast_in_dim x2 -> x0, local copies, waits for them, and re-layouts: 5.47 us -> none  [spread_rows(): jnp.broadcast_to(buffer.reshape(expert_count // 2, 1, capacity, features)...]
    unnamed x21 -> x17, local copies, waits for them, and re-layouts: 3.72 us -> 8.77 us
  transfers between devices with their start and end apart: 8 -> 0, of which waited for: 6 -> 0; matrix products, arithmetic and copies ran while one was open for 16% -> 0% of each run, Pallas kernels for 0% -> 0%
where the time goes in v1:
time: 177 us; the launch traced here: 174 us
  Pallas kernels  165 us (93%)
  local copies, waits for them, and re-layouts  8.77 us (5%)
    pallas_call x1, Pallas kernels, on_device(): pl.pallas_call(kernel, out_shape=(jax.ShapeDtypeStruct((ntok, features),...  165 us
    unnamed x17, local copies, waits for them, and re-layouts  8.77 us

profile of v1, /device:TPU:14, one launch (start us, length us, event | category | flops | bytes accessed | tf_op | source)
XLA Modules:
  0.0 174.2 jit_solution(9468524208347974154)
XLA Ops:
  0.6 0.0 copy-start.4
  0.6 1.4 copy.12.ids
  2.0 0.0 copy-done.4
  2.0 0.7 copy.13.gv
  2.8 164.7 %shard_map.110 = (bf16[128,4096]{1,0:T(8,128)(2,1)}, bf16[128,4096]{1,0:T(8,128)(2,1)}, f32[256,384]{1,0:T(8,128)}, f32[256,384]{1,0:T(8,128)}, f32[256,384]{1,0:T(8,128)}) custom-call(bf16[128,4096]{1,0:T(8,128)(2,1)} %tok.1, s32[128,1]{1,0:T(8,128)} %copy.12.ids, f32[128,1]{1,0:T(8,128)} %copy.13.gv, bf16[128,4096]{1,0:T(8,128)(2,1)} %cot.1, ...), custom_call_target="tpu_custom_call" | custom-call | flops 10871635968 | bytes 4194304 | tf_op jit(solution)/shard_map/pallas_call | solution.py:482
  167.5 0.0 copy-start
  167.5 2.4 %copy.19 = bf16[128,4096]{1,0:T(8,128)(2,1)} copy(bf16[128,4096]{1,0:T(8,128)(2,1)} %get-tuple-element.10) | data formatting | bytes 2097152
  169.9 0.0 copy-done
  169.9 0.0 copy-start.3
  169.9 1.0 copy.20
  170.9 0.3 copy-done.3
  171.1 0.0 copy-start.2
  171.1 0.7 copy.21
  171.9 0.4 copy-done.2
  172.3 0.0 copy-start.1
  172.3 0.7 copy.22
  173.0 0.4 copy-done.1
  173.4 0.7 copy.23
Async XLA Ops:
  0.6 1.4 copy-start.4
  167.5 2.4 %copy-start = (bf16[128,4096]{1,0:T(8,128)(2,1)S(1)}, bf16[128,4096]{1,0:T(8,128)(2,1)}, u32[]{:S(2)}) copy-start(bf16[128,4096]{1,0:T(8,128)(2,1)} %get-tuple-element.11) | copy-start | bytes 3145732
  169.9 1.2 copy-start.3
  171.1 1.1 copy-start.2
  172.3 1.1 copy-start.1

commit v2 on v1

v2 whole, which is shorter than its diff:
```python
import jax
import jax.numpy as jnp
from jax import lax
from jax.experimental import pallas as pl
from jax.experimental.pallas import tpu as pltpu
from jax.sharding import PartitionSpec as P

MESH = pl.DeviceIdType.MESH
BF, F32 = jnp.bfloat16, jnp.float32
HOPS = ({1: 4, -1: 3}, {1: 3, -1: 4}, {1: 4, -1: 3})
OWN, PAR, NBR, FWD = 0, 1, 2, 3
MIRROR = (PAR, OWN, FWD, NBR)
CAP = 24
SLAB = 2 * CAP
BLK = 256
N_SEM = 170


def kernel(
    tok_hbm, ids, gv, cot_hbm, wg, wu, wd,
    o_moe, o_tok, o_gate, o_up, o_down,
    tok, cot, wgr, w_all, dw,
    s_t, own_t, oth_t, par_t, nbr_t, fwd_t, s_c, own_c, oth_c, par_c, nbr_c, fwd_c,
    x_buf, g_buf, x_t, g_t, out_own, out_nbr, out_par, out_fwd, out_oth, out_res,
    part, back_own, back_nbr, back_oth, res, sib_buf, ring_buf,
    pre, act, hid, hid_in, gh_out, gh_in, swap_out, swap_in, sel, ssem, rsem, lsem,
):
    nz = w_all.shape[1]
    units = wg.shape[1]
    half = s_t.shape[-1]
    quarter = half // 2
    rows = x_buf.shape[0]
    group = rows // 4
    ntok = ids.shape[1]
    dp, ex = lax.axis_index("dp"), lax.axis_index("expert")
    z, c = lax.div(dp, 2), lax.rem(dp, 2)
    y, x = lax.div(ex, 4), lax.rem(ex, 4)
    p, hh = lax.div(x, 2), lax.rem(x, 2)
    partner = (dp, ex + 1 - 2 * hh)
    neighbour = (dp, y * 4 + 3 - x)
    sibling = (dp + 1 - 2 * c, ex)
    diagonal = (dp + 1 - 2 * c, ex + 1 - 2 * hh)
    swapped = c != hh

    def zpos(off):
        return lax.rem(z + nz + off, nz)

    def zdev(d):
        return (zpos(d) * 2 + c, ex)

    def ydev(r):
        return (dp, lax.rem(y + r, 4) * 4 + x)

    def expert_at(r, other):
        mine = lax.rem(y + r, 4) * 2 + p
        return mine + (1 - 2 * p) if other else mine

    def cols(m):
        return slice(m * units, (m + 1) * units)

    def block(j):
        return pl.ds(pl.multiple_of(j * BLK, BLK), BLK)

    shards = (wg, wu, wd)
    my_shard = [w_all.at[c, z, :, cols(m)] for m in range(3)]
    load_tok = pltpu.make_async_copy(tok_hbm, tok, lsem.at[0])
    load_cot = pltpu.make_async_copy(cot_hbm, cot, lsem.at[1])
    load_w = [pltpu.make_async_copy(shards[m], my_shard[m], lsem.at[2 + m]) for m in range(3)]
    load_tok.start()
    load_cot.start()

    barrier = pltpu.get_barrier_semaphore()
    for dev in (
        partner, neighbour, sibling, diagonal, zdev(1), zdev(-1), ydev(1), ydev(2), ydev(3)
    ):
        pl.semaphore_signal(barrier, inc=1, device_id=dev, device_id_type=MESH)
    pl.semaphore_wait(barrier, 9)

    copies, received, sent = {}, set(), set()

    def remote(key, src, dst, dev):
        i = len(copies)
        copies[key] = pltpu.make_async_remote_copy(
            src_ref=src, dst_ref=dst, send_sem=ssem.at[i], recv_sem=rsem.at[i],
            device_id=dev, device_id_type=MESH,
        )
        return copies[key]

    def send(key, src, dst, dev):
        remote(key, src, dst, dev).start()

    def got(*key):
        if key not in received:
            received.add(key)
            copies[key].wait_recv()

    def drain(*kinds):
        for key, copy in copies.items():
            if key not in sent and (not kinds or key[0] in kinds):
                sent.add(key)
                copy.wait_send()

    def w_start(m):
        src = shards[m] if m < 2 else my_shard[m]
        for d in (1, -1):
            send(("w", m, d, 1), src, my_shard[m], zdev(d))

    def w_share(m):
        send(("ws", m, 0, 0), shards[m] if m < 2 else my_shard[m], my_shard[m], sibling)

    def w_arrive(m, s):
        for d in (1, -1):
            if s <= HOPS[m][d]:
                got("w", m, d, s)
                piece = w_all.at[c, zpos(-d * s), :, cols(m)]
                if s < HOPS[m][d]:
                    send(("w", m, d, s + 1), piece, piece, zdev(d))
                send(("ws", m, d, s), piece, piece, sibling)

    def w_ready(m):
        for d in (1, -1):
            for s in range(1, HOPS[m][d] + 1):
                got("w", m, d, s)
                got("ws", m, d, s)
        got("ws", m, 0, 0)
        if m < 2:
            load_w[m].wait()

    swap = remote(("swap",), wd, w_all.at[1 - c, z, :, cols(2)], diagonal)
    sent.add(("swap",))
    received.add(("swap",))

    def swap_start():
        @pl.when(swapped)
        def _():
            swap.start()

        @pl.when(jnp.logical_not(swapped))
        def _():
            load_w[2].start()

    def swap_wait():
        @pl.when(swapped)
        def _():
            swap.wait_recv()
            swap.wait_send()

        @pl.when(jnp.logical_not(swapped))
        def _():
            load_w[2].wait()

    def slots():
        lane = lax.broadcasted_iota(jnp.int32, (ntok, ntok), 1)
        down = lax.broadcasted_iota(jnp.int32, (ntok, ntok), 0)
        eye = down == lane
        idv = jnp.sum(
            jnp.where(eye, ids[...].astype(F32), 0.0), axis=1, keepdims=True
        ).astype(jnp.int32)
        gate = jnp.sum(jnp.where(eye, gv[...], 0.0), axis=1, keepdims=True)
        onehot = jnp.where(idv == lane, 1.0, 0.0).astype(F32)
        lower = jnp.where(down > lane, 1.0, 0.0).astype(BF)
        before = jnp.dot(lower, onehot.astype(BF), preferred_element_type=F32)
        order = jnp.sum(before * onehot, axis=1, keepdims=True).astype(jnp.int32)
        place = idv * SLAB + order
        slot = lax.broadcasted_iota(jnp.int32, (ntok, sel.shape[2]), 1)
        for k in range(2):
            sel[k] = jnp.where(slot == place + k * CAP, 1.0, 0.0).astype(BF)
        return gate

    by_rows = (((0,), (0,)), ((), ()))
    by_cols = (((1,), (1,)), ((), ()))

    def spread(k, source, at):
        return lax.dot_general(sel[k], source(at), by_rows, preferred_element_type=F32)

    def dispatch_t():
        def body(j, carry):
            acc = spread(0, lambda at: tok[:, at], block(2 * j))
            acc = acc + spread(1, lambda at: tok[:, at], block(2 * j + 1))
            s_t[:, :, block(j)] = acc.astype(BF).reshape(8, SLAB, BLK)
            return carry

        lax.fori_loop(0, nz, body, 0)

    def dispatch_c(gate):
        def scaled(at):
            return (gate * cot[:, at].astype(F32)).astype(BF)

        def body(j, carry):
            for h in range(2):
                acc = spread(0, scaled, block(2 * j + h))
                acc = acc + spread(1, scaled, block(2 * (j + nz // 2) + h))
                s_c[:, h, :, block(j)] = acc.astype(BF).reshape(8, SLAB, BLK)
            return carry

        lax.fori_loop(0, nz // 2, body, 0)

    stores = {"t": (s_t, own_t, oth_t, par_t, nbr_t, fwd_t), "c": (s_c, own_c, oth_c, par_c, nbr_c, fwd_c)}

    def theirs(ph, ref):
        return ref if ph == "t" else ref.at[1 - hh]

    def y_own(ph, *hops):
        for r in hops:
            s, own = stores[ph][0], stores[ph][1]
            send(("own", ph, r), s.at[expert_at(r, False)], own.at[r - 1], ydev(r))

    def y_oth(ph, *hops):
        for r in hops:
            s, oth = stores[ph][0], stores[ph][2]
            send(("oth", ph, r), s.at[expert_at(r, True)], oth.at[r - 1], ydev(r))

    def self_par(ph):
        s, par = stores[ph][0], stores[ph][3]
        send(("par", ph, 0), theirs(ph, s.at[expert_at(0, False)]), par.at[0], partner)

    def self_nbr(ph):
        s, nbr = stores[ph][0], stores[ph][4]
        send(("nbr", ph, 0), s.at[expert_at(0, True)], nbr.at[0], neighbour)

    def t_own(ph, r):
        got("own", ph, r)
        own, par = stores[ph][1], stores[ph][3]
        send(("par", ph, r), theirs(ph, own.at[r - 1]), par.at[r], partner)

    def t_oth(ph, r):
        got("oth", ph, r)
        oth, nbr = stores[ph][2], stores[ph][4]
        send(("nbr", ph, r), oth.at[r - 1], nbr.at[r], neighbour)

    def t_nbr(ph, r):
        got("nbr", ph, r)
        nbr, fwd = stores[ph][4], stores[ph][5]
        send(("fwd", ph, r), theirs(ph, nbr.at[r]), fwd.at[r], partner)

    wide = 512

    def gather_rows(ph):
        s, own, oth, par, nbr, fwd = stores[ph]
        for r in range(4):
            got("par", ph, r)
            got("fwd", ph, r)

        def slab(g, r, at):
            if g == OWN:
                ref = s.at[expert_at(0, False)] if r == 0 else own.at[r - 1]
            else:
                ref = (None, par, nbr, fwd)[g].at[r]
            if ph == "c" and g in (OWN, NBR):
                ref = ref.at[hh]
            return ref[:, at].astype(F32)

        to_buf, width = (x_buf, half) if ph == "t" else (g_buf, quarter)

        def body(j, carry):
            at = pl.ds(pl.multiple_of(j * wide, wide), wide)
            for g in range(4):
                for r in (0, 2):
                    first, second = slab(g, r, at), slab(g, r + 1, at)
                    base = (g * 4 + r) * CAP
                    for h in range(2):
                        both = jnp.concatenate(
                            [first[h * CAP:(h + 1) * CAP], second[h * CAP:(h + 1) * CAP]], axis=0
                        )
                        to = pl.ds(pl.multiple_of(h * width + j * wide, wide), wide)
                        to_buf[base:base + SLAB, to] = both.astype(BF)
            return carry

        lax.fori_loop(0, width // wide, body, 0)

    def turn(to, source, start, stop):
        def body(j, carry):
            to[block(j), :] = jnp.transpose(source[:, block(j)])
            return carry

        lax.fori_loop(start, stop, body, 0)

    def project_t():
        to = slice(0, 2 * units)
        pre[:, to] = jnp.zeros((rows, 2 * units), F32)

        def body(j, carry):
            acc = None
            for k in range(2):
                term = jnp.dot(
                    x_buf[:, block(k * nz + j)], w_all[k, j, :, to], preferred_element_type=F32
                )
                acc = term if acc is None else acc + term
            pre[:, to] += acc
            return carry

        lax.fori_loop(0, nz, body, 0)

    def project_c():
        pre[:, 2 * units:] = jnp.zeros((rows, 2 * units), F32)

        def body(j, carry):
            for k in range(2):
                acc = None
                for i in range(2):
                    term = jnp.dot(
                        g_buf[:, block(2 * j + i)], w_all[k, 2 * j + i, :, cols(2)],
                        preferred_element_type=F32,
                    )
                    acc = term if acc is None else acc + term
                pre[:, cols(2 + k)] += acc
            return carry

        lax.fori_loop(0, nz // 2, body, 0)

        def pick(at, want):
            low = (want == 0).astype(F32)
            return pre[at, cols(2)] * low + pre[at, cols(3)] * (1.0 - low)

        def split(i, carry):
            at = pl.ds(pl.multiple_of(i * tall, tall), tall)
            gh_out[at, :] = pick(at, 1 - hh).astype(BF)
            pre[at, cols(2)] = pick(at, hh)
            return carry

        lax.fori_loop(0, rows // tall, split, 0)
        send(("gh",), gh_out, gh_in, partner)

    tall = 32

    def activate():
        def body(i, carry):
            at = pl.ds(pl.multiple_of(i * tall, tall), tall)
            gate, up = pre[at, cols(0)], pre[at, cols(1)]
            hid[hh, at, :] = (gate * jax.nn.sigmoid(gate) * up).astype(BF)
            return carry

        lax.fori_loop(0, rows // tall, body, 0)
        send(("hid",), hid.at[hh], hid_in, partner)

    def join_hidden():
        got("hid")
        for g in range(4):
            m = MIRROR[g]
            hid[1 - hh, g * group:(g + 1) * group, :] = hid_in[m * group:(m + 1) * group, :]

    def differentiate():
        got("gh")
        for g in range(4):
            def body(i, carry, g=g):
                at = pl.ds(pl.multiple_of(g * group + i * tall, tall), tall)
                there = pl.ds(pl.multiple_of(MIRROR[g] * group + i * tall, tall), tall)
                gate, up = pre[at, cols(0)], pre[at, cols(1)]
                grad = pre[at, cols(2)] + gh_in[there, :].astype(F32)
                sig = jax.nn.sigmoid(gate)
                act[at, cols(0)] = (grad * up * sig * (1.0 + gate * (1.0 - sig))).astype(BF)
                act[at, cols(1)] = (grad * (gate * sig)).astype(BF)
                return carry

            lax.fori_loop(0, group // tall, body, 0)

    def slabs(first, second):
        shape = (rows // CAP, CAP, BLK)
        joined = jnp.concatenate([first.reshape(shape), second.reshape(shape)], axis=1)
        return joined.astype(BF).reshape(4, 4, SLAB, BLK)

    def outputs():
        def body(j, carry):
            both = []
            for q in range(2):
                value = None
                for k in range(2):
                    term = lax.dot_general(
                        hid[k], w_all[k, j + q * (nz // 2), :, cols(2)], by_cols,
                        preferred_element_type=F32,
                    )
                    value = term if value is None else value + term
                both.append(value)
            joined = slabs(*both)
            out_own[:, hh, :, block(j)] = joined[OWN]
            out_nbr[:, hh, :, block(j)] = joined[NBR]
            out_par[:, :, block(j)] = joined[PAR]
            out_fwd[:, :, block(j)] = joined[FWD]
            return carry

        lax.fori_loop(0, nz // 2, body, 0)

    def row_grads():
        def body(j, carry):
            both = [
                lax.dot_general(
                    act[...], w_all[k, j, :, 0:2 * units], by_cols, preferred_element_type=F32
                )
                for k in range(2)
            ]
            part[:, :, :, block(j)] = slabs(*both)
            return carry

        lax.fori_loop(0, nz, body, 0)

    queue = []
    for turn_of in ("o", "g"):
        for kind in ("bn", "bo"):
            queue += [(kind, turn_of, r) for r in (2, 1, 3, 0)]

    def feed(count):
        for _ in range(count):
            kind, ph, r = queue.pop(0)
            if ph == "o":
                pairs = {"bn": (out_fwd.at[r], out_nbr.at[r, hh]), "bo": (out_par.at[r], out_own.at[r, hh])}
            else:
                pairs = {"bn": (part.at[FWD, r], back_nbr.at[r]), "bo": (part.at[PAR, r], back_own.at[r])}
            send((kind, ph, r), *pairs[kind], partner)

    def add_into(dst, a, b):
        def body(j, carry):
            at = pl.ds(pl.multiple_of(j * wide, wide), wide)
            dst[:, at] = (a[:, at].astype(F32) + b[:, at].astype(F32)).astype(BF)
            return carry

        lax.fori_loop(0, half // wide, body, 0)

    def back_n(ph, r):
        got("bn", ph, r)
        if ph == "o":
            mine, oth = out_nbr.at[r], out_oth
        else:
            mine, oth = part.at[NBR, r], back_oth
            add_into(mine, mine, back_nbr.at[r])
        send(("bx", ph, r), mine, oth.at[r], neighbour)

    def back_o(ph, r):
        got("bo", ph, r)
        e = expert_at(0, False)
        if ph == "o":
            mine, to = out_own.at[r], out_res.at[e]
            if r == 0:
                out_res[e] = out_own[0]
        else:
            mine, to = part.at[OWN, r], res.at[e]
            add_into(to if r == 0 else mine, mine, back_own.at[r])
        if r > 0:
            send(("ro", ph, r), mine, to, ydev(4 - r))

    def back_x(ph, r):
        got("bx", ph, r)
        e = expert_at(0, True)
        oth, to = (out_oth, out_res) if ph == "o" else (back_oth, res)
        if r == 0:
            to[e] = oth[0]
        else:
            send(("rx", ph, r), oth.at[r], to.at[e], ydev(4 - r))

    def combine_o(gate):
        for r in (1, 2, 3):
            got("ro", "o", r)
            got("rx", "o", r)

        def body(j, carry):
            for h in range(2):
                back = out_res[:, h, :, block(j)].reshape(8 * SLAB, BLK)
                for q in range(2):
                    value = gate * jnp.dot(sel[q], back, preferred_element_type=F32)
                    tok[:, block(2 * (j + q * (nz // 2)) + h)] = value.astype(BF)
            return carry

        lax.fori_loop(0, nz // 2, body, 0)
        store(0, tok, o_moe)

    def combine_g():
        for r in (1, 2, 3):
            got("ro", "g", r)
            got("rx", "g", r)

        def body(j, carry):
            back = res[:, :, block(j)].reshape(8 * SLAB, BLK)
            for h in range(2):
                value = jnp.dot(sel[h], back, preferred_element_type=F32)
                cot[:, block(2 * j + h)] = value.astype(BF)
            return carry

        lax.fori_loop(0, nz, body, 0)
        store(1, cot, o_tok)

    def grad_at(m, k, zz):
        ref = w_all if m == 2 else dw
        return ref.at[k, zz, :, cols(m)]

    ORDER = (4, 3, 5, 2, 6, 1, 7, 0)

    def offset(j):
        odd = lax.rem(j, 2)
        return 4 + lax.div(j, 2) * (1 - odd) - lax.div(j + 1, 2) * odd

    def weight_grads(kind, k, to_sibling):
        to, at_cols = (w_all, cols(2)) if kind == "d" else (dw, slice(0, 2 * units))
        base = len(copies)

        def piece(j, off):
            return pltpu.make_async_remote_copy(
                src_ref=to.at[k, zpos(off), :, at_cols], dst_ref=sib_buf.at[off, :, at_cols],
                send_sem=ssem.at[base + j], recv_sem=rsem.at[base + j],
                device_id=sibling, device_id_type=MESH,
            )

        def body(j, carry):
            off = offset(j)
            zz = zpos(off)
            if kind == "d":
                value = jnp.dot(g_t[block(zz), :], hid[k], preferred_element_type=F32)
            else:
                value = jnp.dot(
                    x_t[block(k * nz + zz), :], act[...], preferred_element_type=F32
                )
            to[k, zz, :, at_cols] = value.astype(BF)
            if to_sibling:
                piece(j, off).start()
            return carry

        lax.fori_loop(0, nz, body, 0)
        if to_sibling:
            for j, off in enumerate(ORDER):
                copies["sib", kind, off] = piece(j, off)

    ring_slots = {}

    def slot_of(*key):
        return ring_buf.at[ring_slots.setdefault(key, len(ring_slots))]

    def local_sum(m, off):
        got("sib", "d" if m == 2 else "gu", off)
        mine = grad_at(m, c, zpos(off))
        return mine[...].astype(F32) + sib_buf[off, :, cols(m)].astype(F32)

    def ring_send(m, s):
        for d in (1, -1):
            hops = HOPS[m][d]
            if s < hops:
                off = (d * (hops - s)) % nz
                total = local_sum(m, off)
                if s > 0:
                    got("ring", m, d, s - 1)
                    total = total + slot_of(m, d, s - 1)[...].astype(F32)
                piece = grad_at(m, c, zpos(off))
                piece[...] = total.astype(BF)
                send(("ring", m, d, s), piece, slot_of(m, d, s), zdev(d))

    def ring_total(m):
        total = local_sum(m, 0)
        for d in (1, -1):
            last = HOPS[m][d] - 1
            got("ring", m, d, last)
            total = total + slot_of(m, d, last)[...].astype(F32)
        return total

    def ring_end(m):
        wgr[m] = ring_total(m)
        store(2 + m, wgr.at[m], (o_gate, o_up)[m])

    def ring_end_down():
        wgr[2] = ring_total(2)
        back = remote(("back",), swap_out, swap_in, diagonal)
        sent.add(("back",))
        received.add(("back",))

        @pl.when(swapped)
        def _():
            swap_out[...] = wgr[2].astype(BF)
            back.start()

        return back

    def down_done(back):
        @pl.when(swapped)
        def _():
            back.wait_recv()
            back.wait_send()
            wgr[2] = swap_in[...].astype(F32)

        store(4, wgr.at[2], o_down)

    stored = []

    def store(i, src, dst):
        stored.append(pltpu.make_async_copy(src, dst, lsem.at[5 + i]))
        stored[-1].start()

    def ring(*steps):
        for m, s in steps:
            ring_send(m, s)

    w_start(0)
    w_start(1)
    swap_start()
    w_share(0)
    w_share(1)
    load_w[0].start()
    load_w[1].start()
    gate_col = slots()
    load_tok.wait()
    dispatch_t()
    self_par("t")
    self_nbr("t")
    y_own("t", 1, 3)
    load_cot.wait()
    dispatch_c(gate_col)
    t_own("t", 1)
    t_own("t", 3)
    y_oth("t", 1, 3, 2)
    t_nbr("t", 0)
    w_arrive(0, 1)
    w_arrive(1, 1)
    t_oth("t", 1)
    t_oth("t", 3)
    y_own("t", 2)
    w_arrive(0, 2)
    t_oth("t", 2)
    t_nbr("t", 1)
    w_arrive(1, 2)
    t_nbr("t", 3)
    t_own("t", 2)
    y_own("c", 1, 3)
    w_arrive(0, 3)
    self_nbr("c")
    t_nbr("t", 2)
    w_arrive(1, 3)
    swap_wait()
    w_start(2)
    w_share(2)
    y_oth("c", 1, 3, 2)
    self_par("c")
    w_arrive(0, 4)
    w_arrive(1, 4)
    t_own("c", 1)
    t_own("c", 3)
    t_oth("c", 1)
    t_oth("c", 3)
    y_own("c", 2)
    t_nbr("c", 0)
    gather_rows("t")
    w_arrive(2, 1)
    t_oth("c", 2)
    w_ready(0)
    w_ready(1)
    project_t()
    activate()
    t_own("c", 2)
    t_nbr("c", 1)
    t_nbr("c", 3)
    w_arrive(2, 2)
    t_nbr("c", 2)
    turn(x_t, x_buf, 0, nz)
    w_arrive(2, 3)
    turn(x_t, x_buf, nz, 2 * nz)
    w_arrive(2, 4)
    w_ready(2)
    gather_rows("c")
    project_c()
    drain("w", "ws")
    turn(g_t, g_buf, 0, nz)
    join_hidden()
    outputs()
    weight_grads("d", 1 - c, True)
    weight_grads("d", c, False)
    ring((2, 0))
    got("gh")
    feed(5)
    differentiate()
    weight_grads("gu", 1 - c, True)
    ring((2, 1))
    back_n("o", 2)
    back_n("o", 1)
    weight_grads("gu", c, False)
    ring((0, 0), (1, 0))
    feed(3)
    row_grads()
    feed(2)
    back_n("o", 3)
    back_n("o", 0)
    ring((2, 2))
    back_x("o", 2)
    back_x("o", 1)
    back_o("o", 2)
    back_o("o", 1)
    back_o("o", 3)
    back_x("o", 3)
    ring((0, 1), (1, 1))
    feed(1)
    back_o("o", 0)
    back_x("o", 0)
    back_n("g", 2)
    feed(1)
    ring((2, 3))
    back_n("g", 1)
    feed(1)
    back_x("g", 2)
    ring((0, 2), (1, 2))
    back_n("g", 3)
    feed(1)
    back_x("g", 1)
    combine_o(gate_col)
    back_n("g", 0)
    feed(1)
    back_x("g", 3)
    swapping = ring_end_down()
    back_o("g", 2)
    feed(1)
    back_x("g", 0)
    ring((0, 3), (1, 3))
    back_o("g", 1)
    down_done(swapping)
    back_o("g", 3)
    ring_end(0)
    ring_end(1)
    back_o("g", 0)
    combine_g()
    drain()
    for copy in stored:
        copy.wait()


def finish(*refs):
    ins, outs, held, sems = refs[0:5], refs[5:10], refs[10:15], refs[15]
    loads = [pltpu.make_async_copy(a, b, sems.at[i]) for i, (a, b) in enumerate(zip(ins, held))]
    moves = [pltpu.make_async_copy(a, b, sems.at[5 + i]) for i, (a, b) in enumerate(zip(held, outs))]
    for load in loads:
        load.start()
    for load, move in zip(loads, moves):
        load.wait()
        move.start()
    for move in moves:
        move.wait()


def on_device(tokens, expert_ids, gate_values, cotangent, gate_weight, up_weight, down_weight):
    ntok, features = tokens.shape
    depth, units = gate_weight.shape
    nz = lax.axis_size("dp") // 2
    half = features // 2
    rows = 16 * CAP
    slab = (SLAB, half)
    small = (SLAB, half // 2)
    pair = (2,) + small
    shapes = (
        jax.ShapeDtypeStruct((ntok, features), BF),
        jax.ShapeDtypeStruct((ntok, features), BF),
        jax.ShapeDtypeStruct((depth, units), F32),
        jax.ShapeDtypeStruct((depth, units), F32),
        jax.ShapeDtypeStruct((depth, units), F32),
    )
    hbm, vmem = pl.BlockSpec(memory_space=pl.ANY), pl.BlockSpec(memory_space=pltpu.VMEM)
    results = pl.pallas_call(
        kernel,
        out_shape=shapes,
        in_specs=[hbm, vmem, vmem, hbm, hbm, hbm, hbm],
        out_specs=(hbm,) * 5,
        scratch_shapes=[
            pltpu.VMEM((ntok, features), BF),
            pltpu.VMEM((ntok, features), BF),
            pltpu.VMEM((3, depth, units), F32),
            pltpu.VMEM((2, nz, depth, 3 * units), BF),
            pltpu.VMEM((2, nz, depth, 2 * units), BF),
            pltpu.VMEM((8,) + slab, BF),
            pltpu.VMEM((3,) + slab, BF),
            pltpu.VMEM((3,) + slab, BF),
            pltpu.VMEM((4,) + slab, BF),
            pltpu.VMEM((4,) + slab, BF),
            pltpu.VMEM((4,) + slab, BF),
            pltpu.VMEM((8,) + pair, BF),
            pltpu.VMEM((3,) + pair, BF),
            pltpu.VMEM((3,) + pair, BF),
            pltpu.VMEM((4,) + small, BF),
            pltpu.VMEM((4,) + pair, BF),
            pltpu.VMEM((4,) + small, BF),
            pltpu.VMEM((rows, features), BF),
            pltpu.VMEM((rows, half), BF),
            pltpu.VMEM((features, rows), BF),
            pltpu.VMEM((half, rows), BF),
            pltpu.VMEM((4,) + pair, BF),
            pltpu.VMEM((4,) + pair, BF),
            pltpu.VMEM((4,) + small, BF),
            pltpu.VMEM((4,) + small, BF),
            pltpu.VMEM((4,) + pair, BF),
            pltpu.VMEM((8,) + pair, BF),
            pltpu.VMEM((4, 4) + slab, BF),
            pltpu.VMEM((4,) + slab, BF),
            pltpu.VMEM((4,) + slab, BF),
            pltpu.VMEM((4,) + slab, BF),
            pltpu.VMEM((8,) + slab, BF),
            pltpu.VMEM((nz, depth, 3 * units), BF),
            pltpu.VMEM((21, depth, units), BF),
            pltpu.VMEM((rows, 4 * units), F32),
            pltpu.VMEM((rows, 2 * units), BF),
            pltpu.VMEM((2, rows, units), BF),
            pltpu.VMEM((rows, units), BF),
            pltpu.VMEM((rows, units), BF),
            pltpu.VMEM((rows, units), BF),
            pltpu.VMEM((depth, units), BF),
            pltpu.VMEM((depth, units), BF),
            pltpu.VMEM((2, ntok, 8 * SLAB), BF),
            pltpu.SemaphoreType.DMA((N_SEM,)),
            pltpu.SemaphoreType.DMA((N_SEM,)),
            pltpu.SemaphoreType.DMA((10,)),
        ],
        compiler_params=pltpu.CompilerParams(
            collective_id=0, has_side_effects=True, vmem_limit_bytes=62 * 1024 * 1024
        ),
        cost_estimate=pl.CostEstimate(
            flops=18 * rows * features * units, bytes_accessed=8 * ntok * features,
            transcendentals=2 * rows * units,
        ),
    )(
        tokens, expert_ids.reshape(1, ntok), gate_values.reshape(1, ntok), cotangent,
        gate_weight, up_weight, down_weight,
    )
    return pl.pallas_call(
        finish,
        out_shape=shapes,
        in_specs=[hbm] * 5,
        out_specs=(hbm,) * 5,
        scratch_shapes=[pltpu.VMEM(a.shape, a.dtype) for a in shapes]
        + [pltpu.SemaphoreType.DMA((10,))],
        compiler_params=pltpu.CompilerParams(vmem_limit_bytes=62 * 1024 * 1024),
    )(*results)


def solution(mesh):
    rows, weights = P(("dp", "expert"), None), P("dp", "expert")
    return jax.shard_map(
        on_device,
        mesh=mesh,
        in_specs=(rows, rows, rows, rows, weights, weights, weights),
        out_specs=(rows, rows, weights, weights, weights),
        check_vma=False,
    )
```

time: 177 us -> 148 us (0.84); the launches traced: 174 us -> 148 us
  Pallas kernels: 165 us -> 147 us
  local copies, waits for them, and re-layouts: 8.77 us -> 0 us
    pallas_call x1 -> x2, Pallas kernels: 165 us -> 147 us  [the longest x1 144 us: on_device(): pl.pallas_call(kernel, out_shape=shapes, in_specs=[hbm, vmem, vmem, hbm,...]
    unnamed x17 -> x0, local copies, waits for them, and re-layouts: 8.77 us -> none
where the time goes in v2:
time: 148 us
  Pallas kernels  147 us (99%)
    pallas_call x1, Pallas kernels, on_device(): pl.pallas_call(kernel, out_shape=shapes, in_specs=[hbm, vmem, vmem, hbm,...  144 us
    pallas_call x1, Pallas kernels, on_device(): pl.pallas_call(finish, out_shape=shapes, in_specs=[hbm] * 5, out_specs=(h...  3.01 us

profile of v2, /device:TPU:14, one launch (start us, length us, event | category | flops | bytes accessed | tf_op | source)
XLA Modules:
  0.0 148.1 jit_solution(6836989204793211084)
XLA Ops:
  0.6 144.4 %shard_map.110 = (bf16[128,4096]{1,0:T(8,128)(2,1)}, bf16[128,4096]{1,0:T(8,128)(2,1)}, f32[256,384]{1,0:T(8,128)}, f32[256,384]{1,0:T(8,128)}, f32[256,384]{1,0:T(8,128)}) custom-call(bf16[128,4096]{1,0:T(8,128)(2,1)} %tok_hbm.1, s32[1,128]{1,0:T(1,128)} %bitcast.2, f32[1,128]{1,0:T(1,128)} %bitcast.3, bf16[128,4096]{1,0:T(8,128)(2,1)} %cot_hbm.1, ...), custom_call_target="tpu_custom_call" | custom-call | flops 10871635968 | bytes 4194304 | tf_op jit(solution)/shard_map/pallas_call | solution.py:747
  145.1 3.0 %shard_map.111 = (bf16[128,4096]{1,0:T(8,128)(2,1)}, bf16[128,4096]{1,0:T(8,128)(2,1)}, f32[256,384]{1,0:T(8,128)}, f32[256,384]{1,0:T(8,128)}, f32[256,384]{1,0:T(8,128)}) custom-call(bf16[128,4096]{1,0:T(8,128)(2,1)} %get-tuple-element.10.refs_0_, bf16[128,4096]{1,0:T(8,128)(2,1)} %get-tuple-element.11.refs_1_, f32[256,384]{1,0:T(8,128)} %get-tuple-element.12.refs_2_, ...), custom_call_target="tpu_custom_call" | custom-call | tf_op jit(solution)/shard_map/pallas_call | solution.py:811

commit v3 on v2

--- a/solution.py
+++ b/solution.py
@@ -1,3 +1,5 @@
+import math
+
 import jax
 import jax.numpy as jnp
 from jax import lax
@@ -13,17 +15,17 @@
 CAP = 24
 SLAB = 2 * CAP
 BLK = 256
-N_SEM = 170
+N_SEND, N_RECV = 14, 123
 
 
 def kernel(
     tok_hbm, ids, gv, cot_hbm, wg, wu, wd,
-    o_moe, o_tok, o_gate, o_up, o_down,
-    tok, cot, wgr, w_all, dw,
+    o_moe, o_res, o_sel, o_gate, o_up, o_down,
+    tok, cot, w_all, dw,
     s_t, own_t, oth_t, par_t, nbr_t, fwd_t, s_c, own_c, oth_c, par_c, nbr_c, fwd_c,
     x_buf, g_buf, x_t, g_t, out_own, out_nbr, out_par, out_fwd, out_oth, out_res,
     part, back_own, back_nbr, back_oth, res, sib_buf, ring_buf,
-    pre, act, hid, hid_in, gh_out, gh_in, swap_out, swap_in, sel, ssem, rsem, lsem,
+    pre, act, hid, hid_in, gh_out, gh_in, swap_out, swap_in, sel, sel_t, ssem, rsem, lsem,
 ):
     nz = w_all.shape[1]
     units = wg.shape[1]
@@ -76,29 +78,65 @@
         pl.semaphore_signal(barrier, inc=1, device_id=dev, device_id_type=MESH)
     pl.semaphore_wait(barrier, 9)
 
-    copies, received, sent = {}, set(), set()
+    copies, sizes, received, sent = {}, {}, set(), set()
+    send_slots, recv_slots = {}, {}
+
+    def send_group(key):
+        if key[0] in ("own", "oth", "par", "nbr", "fwd"):
+            return ("rows", key[1])
+        if key[0] in ("bn", "bo", "bx", "ro", "rx"):
+            return ("back", key[1])
+        if key[0] in ("hid", "gh"):
+            return ("units",)
+        return key[:2] if key[0] in ("ws", "sib") else key[:1]
+
+    def recv_group(key):
+        if key[0] in ("par", "fwd"):
+            return ("pair", key[1])
+        return key[:2] if key[0] == "ws" else key
+
+    def numbered(slots, name):
+        return slots.setdefault(name, len(slots))
 
     def remote(key, src, dst, dev):
-        i = len(copies)
+        i, j = numbered(send_slots, send_group(key)), numbered(recv_slots, recv_group(key))
         copies[key] = pltpu.make_async_remote_copy(
-            src_ref=src, dst_ref=dst, send_sem=ssem.at[i], recv_sem=rsem.at[i],
+            src_ref=src, dst_ref=dst, send_sem=ssem.at[i], recv_sem=rsem.at[j],
             device_id=dev, device_id_type=MESH,
         )
+        sizes[key] = src.shape
         return copies[key]
 
     def send(key, src, dst, dev):
         remote(key, src, dst, dev).start()
 
+    piece_size = math.prod(ring_buf.shape[1:])
+
+    def together(keys, i, j):
+        total = sum(math.prod(sizes[k]) for k in keys)
+        assert total % piece_size == 0
+        ref = ring_buf.at[0:total // piece_size]
+        return pltpu.make_async_remote_copy(
+            src_ref=ref, dst_ref=ref, send_sem=ssem.at[i], recv_sem=rsem.at[j],
+            device_id=partner, device_id_type=MESH,
+        )
+
     def got(*key):
-        if key not in received:
-            received.add(key)
-            copies[key].wait_recv()
+        name = recv_group(key)
+        if name not in received:
+            received.add(name)
+            keys = [k for k in copies if recv_group(k) == name]
+            if len(keys) == 1:
+                copies[key].wait_recv()
+            else:
+                together(keys, 0, recv_slots[name]).wait_recv()
 
     def drain(*kinds):
-        for key, copy in copies.items():
-            if key not in sent and (not kinds or key[0] in kinds):
-                sent.add(key)
-                copy.wait_send()
+        for name in send_slots:
+            if name not in sent and (not kinds or name[0] in kinds):
+                sent.add(name)
+                keys = [k for k in copies if send_group(k) == name]
+                together(keys, send_slots[name], 0).wait_send()
 
     def w_start(m):
         src = shards[m] if m < 2 else my_shard[m]
@@ -148,6 +186,12 @@
         @pl.when(jnp.logical_not(swapped))
         def _():
             load_w[2].wait()
+
+    stored = []
+
+    def store(i, src, dst):
+        stored.append(pltpu.make_async_copy(src, dst, lsem.at[5 + i]))
+        stored[-1].start()
 
     def slots():
         lane = lax.broadcasted_iota(jnp.int32, (ntok, ntok), 1)
@@ -164,14 +208,16 @@
         place = idv * SLAB + order
         slot = lax.broadcasted_iota(jnp.int32, (ntok, sel.shape[2]), 1)
         for k in range(2):
-            sel[k] = jnp.where(slot == place + k * CAP, 1.0, 0.0).astype(BF)
+            chosen = jnp.where(slot == place + k * CAP, 1.0, 0.0)
+            sel[k] = chosen.astype(BF)
+            sel_t[k] = jnp.transpose(chosen).astype(BF)
+        store(1, sel, o_sel)
         return gate
 
-    by_rows = (((0,), (0,)), ((), ()))
     by_cols = (((1,), (1,)), ((), ()))
 
     def spread(k, source, at):
-        return lax.dot_general(sel[k], source(at), by_rows, preferred_element_type=F32)
+        return jnp.dot(sel_t[k], source(at), preferred_element_type=F32)
 
     def dispatch_t():
         def body(j, carry):
@@ -462,20 +508,12 @@
         lax.fori_loop(0, nz // 2, body, 0)
         store(0, tok, o_moe)
 
-    def combine_g():
-        for r in (1, 2, 3):
-            got("ro", "g", r)
-            got("rx", "g", r)
-
-        def body(j, carry):
-            back = res[:, :, block(j)].reshape(8 * SLAB, BLK)
-            for h in range(2):
-                value = jnp.dot(sel[h], back, preferred_element_type=F32)
-                cot[:, block(2 * j + h)] = value.astype(BF)
-            return carry
-
-        lax.fori_loop(0, nz, body, 0)
-        store(1, cot, o_tok)
+    def res_out(r):
+        for i, other in enumerate((False, True)):
+            if r > 0:
+                got("rx" if other else "ro", "g", r)
+            e = expert_at(r, other)
+            store(5 + 2 * r + i, res.at[e], o_res.at[e])
 
     def grad_at(m, k, zz):
         ref = w_all if m == 2 else dw
@@ -488,13 +526,15 @@
         return 4 + lax.div(j, 2) * (1 - odd) - lax.div(j + 1, 2) * odd
 
     def weight_grads(kind, k, to_sibling):
+        base = len(recv_slots)
         to, at_cols = (w_all, cols(2)) if kind == "d" else (dw, slice(0, 2 * units))
-        base = len(copies)
+        if to_sibling:
+            first = numbered(send_slots, ("sib", kind))
 
         def piece(j, off):
             return pltpu.make_async_remote_copy(
                 src_ref=to.at[k, zpos(off), :, at_cols], dst_ref=sib_buf.at[off, :, at_cols],
-                send_sem=ssem.at[base + j], recv_sem=rsem.at[base + j],
+                send_sem=ssem.at[first], recv_sem=rsem.at[base + j],
                 device_id=sibling, device_id_type=MESH,
             )
 
@@ -515,7 +555,10 @@
         lax.fori_loop(0, nz, body, 0)
         if to_sibling:
             for j, off in enumerate(ORDER):
-                copies["sib", kind, off] = piece(j, off)
+                key = ("sib", kind, off)
+                numbered(recv_slots, key)
+                copies[key] = piece(j, off)
+                sizes[key] = (w_all.shape[2], units if kind == "d" else 2 * units)
 
     ring_slots = {}
 
@@ -548,19 +591,22 @@
             total = total + slot_of(m, d, last)[...].astype(F32)
         return total
 
+    def done(m):
+        return pre.at[0:w_all.shape[2], cols(m)]
+
     def ring_end(m):
-        wgr[m] = ring_total(m)
-        store(2 + m, wgr.at[m], (o_gate, o_up)[m])
+        done(m)[...] = ring_total(m)
+        store(2 + m, done(m), (o_gate, o_up)[m])
 
     def ring_end_down():
-        wgr[2] = ring_total(2)
+        done(2)[...] = ring_total(2)
         back = remote(("back",), swap_out, swap_in, diagonal)
         sent.add(("back",))
         received.add(("back",))
 
         @pl.when(swapped)
         def _():
-            swap_out[...] = wgr[2].astype(BF)
+            swap_out[...] = done(2)[...].astype(BF)
             back.start()
 
         return back
@@ -570,15 +616,9 @@
         def _():
             back.wait_recv()
             back.wait_send()
-            wgr[2] = swap_in[...].astype(F32)
-
-        store(4, wgr.at[2], o_down)
-
-    stored = []
-
-    def store(i, src, dst):
-        stored.append(pltpu.make_async_copy(src, dst, lsem.at[5 + i]))
-        stored[-1].start()
+            done(2)[...] = swap_in[...].astype(F32)
+
+        store(4, done(2), o_down)
 
     def ring(*steps):
         for m, s in steps:
@@ -679,50 +719,77 @@
     back_o("o", 1)
     back_o("o", 3)
     back_x("o", 3)
-    ring((0, 1), (1, 1))
     feed(1)
     back_o("o", 0)
     back_x("o", 0)
+    ring((0, 1), (1, 1))
     back_n("g", 2)
     feed(1)
-    ring((2, 3))
     back_n("g", 1)
     feed(1)
     back_x("g", 2)
-    ring((0, 2), (1, 2))
+    ring((2, 3))
     back_n("g", 3)
     feed(1)
     back_x("g", 1)
-    combine_o(gate_col)
+    ring((0, 2), (1, 2))
     back_n("g", 0)
     feed(1)
     back_x("g", 3)
-    swapping = ring_end_down()
+    combine_o(gate_col)
     back_o("g", 2)
     feed(1)
     back_x("g", 0)
+    swapping = ring_end_down()
+    back_o("g", 1)
     ring((0, 3), (1, 3))
-    back_o("g", 1)
+    back_o("g", 3)
     down_done(swapping)
-    back_o("g", 3)
     ring_end(0)
     ring_end(1)
+    res_out(1)
+    res_out(2)
     back_o("g", 0)
-    combine_g()
+    res_out(0)
+    res_out(3)
     drain()
     for copy in stored:
         copy.wait()
 
 
-def finish(*refs):
-    ins, outs, held, sems = refs[0:5], refs[5:10], refs[10:15], refs[15]
-    loads = [pltpu.make_async_copy(a, b, sems.at[i]) for i, (a, b) in enumerate(zip(ins, held))]
-    moves = [pltpu.make_async_copy(a, b, sems.at[5 + i]) for i, (a, b) in enumerate(zip(held, outs))]
-    for load in loads:
-        load.start()
-    for load, move in zip(loads, moves):
-        load.wait()
-        move.start()
+def finish(
+    moe_in, res_in, sel_in, gate_in, up_in, down_in,
+    moe_out, tok_out, gate_out, up_out, down_out,
+    moe, res, sel, gate, up, down, tok, lsem, rsem, ssem,
+):
+    count = res.shape[-1] // BLK
+    width = 2 * BLK
+    loads, moves = [], []
+    choose = pltpu.make_async_copy(sel_in, sel, lsem.at[4])
+    choose.start()
+    parts = []
+    for j in range(count):
+        at = pl.ds(j * BLK, BLK)
+        parts.append(pltpu.make_async_copy(res_in.at[:, :, at], res.at[:, :, at], rsem.at[j]))
+        parts[-1].start()
+    whole = ((moe_in, moe, moe_out), (gate_in, gate, gate_out), (up_in, up, up_out), (down_in, down, down_out))
+    for i, (a, v, b) in enumerate(whole):
+        loads.append(pltpu.make_async_copy(a, v, lsem.at[i]))
+        moves.append(pltpu.make_async_copy(v, b, ssem.at[i]))
+        loads[-1].start()
+    choose.wait()
+    for j in range(count):
+        parts[j].wait()
+        rows_back = res[:, :, pl.ds(j * BLK, BLK)].reshape(8 * SLAB, BLK)
+        for h in range(2):
+            value = jnp.dot(sel[h], rows_back, preferred_element_type=F32)
+            tok[:, pl.ds((2 * j + h) * BLK, BLK)] = value.astype(BF)
+        at = pl.ds(j * width, width)
+        moves.append(pltpu.make_async_copy(tok.at[:, at], tok_out.at[:, at], ssem.at[4 + j]))
+        moves[-1].start()
+        if j < 4:
+            loads[j].wait()
+            moves[j].start()
     for move in moves:
         move.wait()
 
@@ -743,16 +810,17 @@
         jax.ShapeDtypeStruct((depth, units), F32),
         jax.ShapeDtypeStruct((depth, units), F32),
     )
+    back = jax.ShapeDtypeStruct((8,) + slab, BF)
+    chosen = jax.ShapeDtypeStruct((2, ntok, 8 * SLAB), BF)
     hbm, vmem = pl.BlockSpec(memory_space=pl.ANY), pl.BlockSpec(memory_space=pltpu.VMEM)
     results = pl.pallas_call(
         kernel,
-        out_shape=shapes,
+        out_shape=(shapes[0], back, chosen) + shapes[2:],
         in_specs=[hbm, vmem, vmem, hbm, hbm, hbm, hbm],
-        out_specs=(hbm,) * 5,
+        out_specs=(hbm,) * 6,
         scratch_shapes=[
             pltpu.VMEM((ntok, features), BF),
             pltpu.VMEM((ntok, features), BF),
-            pltpu.VMEM((3, depth, units), F32),
             pltpu.VMEM((2, nz, depth, 3 * units), BF),
             pltpu.VMEM((2, nz, depth, 2 * units), BF),
             pltpu.VMEM((8,) + slab, BF),
@@ -793,9 +861,10 @@
             pltpu.VMEM((depth, units), BF),
             pltpu.VMEM((depth, units), BF),
             pltpu.VMEM((2, ntok, 8 * SLAB), BF),
-            pltpu.SemaphoreType.DMA((N_SEM,)),
-            pltpu.SemaphoreType.DMA((N_SEM,)),
-            pltpu.SemaphoreType.DMA((10,)),
+            pltpu.VMEM((2, 8 * SLAB, ntok), BF),
+            pltpu.SemaphoreType.DMA((N_SEND,)),
+            pltpu.SemaphoreType.DMA((N_RECV,)),
+            pltpu.SemaphoreType.DMA((18,)),
         ],
         compiler_params=pltpu.CompilerParams(
             collective_id=0, has_side_effects=True, vmem_limit_bytes=62 * 1024 * 1024
@@ -808,13 +877,18 @@
         tokens, expert_ids.reshape(1, ntok), gate_values.reshape(1, ntok), cotangent,
         gate_weight, up_weight, down_weight,
     )
+    held = (shapes[0], back, chosen) + shapes[2:] + (shapes[1],)
     return pl.pallas_call(
         finish,
         out_shape=shapes,
-        in_specs=[hbm] * 5,
+        in_specs=[hbm] * 6,
         out_specs=(hbm,) * 5,
-        scratch_shapes=[pltpu.VMEM(a.shape, a.dtype) for a in shapes]
-        + [pltpu.SemaphoreType.DMA((10,))],
+        scratch_shapes=[pltpu.VMEM(a.shape, a.dtype) for a in held]
+        + [
+            pltpu.SemaphoreType.DMA((5,)),
+            pltpu.SemaphoreType.DMA((nz,)),
+            pltpu.SemaphoreType.DMA((4 + nz,)),
+        ],
         compiler_params=pltpu.CompilerParams(vmem_limit_bytes=62 * 1024 * 1024),
     )(*results)
 

time: 148 us -> 145 us (0.980); the launches traced: 148 us -> 143 us
  Pallas kernels: 147 us -> 142 us
    pallas_call x2, Pallas kernels: 147 us -> 142 us  [the longest x1 138 us: on_device(): pl.pallas_call(kernel, out_shape=(shapes[0], back, chosen) + shapes[2:],...]
where the time goes in v3:
time: 145 us; the launch traced here: 143 us
  Pallas kernels  142 us (98%)
    pallas_call x1, Pallas kernels, on_device(): pl.pallas_call(kernel, out_shape=(shapes[0], back, chosen) + shapes[2:],...  138 us
    pallas_call x1, Pallas kernels, on_device(): pl.pallas_call(finish, out_shape=shapes, in_specs=[hbm] * 6, out_specs=(h...  4.25 us

profile of v3, /device:TPU:14, one launch (start us, length us, event | category | flops | bytes accessed | tf_op | source)
XLA Modules:
  0.0 142.6 jit_solution(8914746118548382125)
XLA Ops:
  0.6 137.7 %shard_map.110 = (bf16[128,4096]{1,0:T(8,128)(2,1)}, bf16[8,48,2048]{2,1,0:T(8,128)(2,1)}, bf16[2,128,384]{2,1,0:T(8,128)(2,1)}, f32[256,384]{1,0:T(8,128)}, f32[256,384]{1,0:T(8,128)}, /*index=5*/f32[256,384]{1,0:T(8,128)}) custom-call(bf16[128,4096]{1,0:T(8,128)(2,1)} %tok_hbm.1, s32[1,128]{1,0:T(1,128)} %bitcast.2, f32[1,128]{1,0:T(1,128)} %bitcast.3, ...), custom_call_target="tpu_custom_call" | custom-call | flops 10871635968 | bytes 4194304 | tf_op jit(solution)/shard_map/pallas_call | solution.py:816
  138.3 4.3 %shard_map.111 = (bf16[128,4096]{1,0:T(8,128)(2,1)}, bf16[128,4096]{1,0:T(8,128)(2,1)}, f32[256,384]{1,0:T(8,128)}, f32[256,384]{1,0:T(8,128)}, f32[256,384]{1,0:T(8,128)}) custom-call(bf16[128,4096]{1,0:T(8,128)(2,1)} %get-tuple-element.11.moe_in, bf16[8,48,2048]{2,1,0:T(8,128)(2,1)} %get-tuple-element.12.res_in, ...), custom_call_target="tpu_custom_call" | custom-call | tf_op jit(solution)/shard_map/pallas_call | solution.py:881

commit v4 on v3

--- a/solution.py
+++ b/solution.py
@@ -15,6 +15,7 @@
 CAP = 24
 SLAB = 2 * CAP
 BLK = 256
+PARTS = 4
 N_SEND, N_RECV = 14, 123
 
 
@@ -76,8 +77,6 @@
         partner, neighbour, sibling, diagonal, zdev(1), zdev(-1), ydev(1), ydev(2), ydev(3)
     ):
         pl.semaphore_signal(barrier, inc=1, device_id=dev, device_id_type=MESH)
-    pl.semaphore_wait(barrier, 9)
-
     copies, sizes, received, sent = {}, {}, set(), set()
     send_slots, recv_slots = {}, {}
 
@@ -624,19 +623,20 @@
         for m, s in steps:
             ring_send(m, s)
 
+    gate_col = slots()
+    load_tok.wait()
+    dispatch_t()
+    pl.semaphore_wait(barrier, 9)
     w_start(0)
     w_start(1)
+    self_par("t")
+    self_nbr("t")
+    y_own("t", 1, 3)
     swap_start()
     w_share(0)
     w_share(1)
     load_w[0].start()
     load_w[1].start()
-    gate_col = slots()
-    load_tok.wait()
-    dispatch_t()
-    self_par("t")
-    self_nbr("t")
-    y_own("t", 1, 3)
     load_cot.wait()
     dispatch_c(gate_col)
     t_own("t", 1)
@@ -645,48 +645,47 @@
     t_nbr("t", 0)
     w_arrive(0, 1)
     w_arrive(1, 1)
+    swap_wait()
+    w_start(2)
+    w_share(2)
     t_oth("t", 1)
     t_oth("t", 3)
     y_own("t", 2)
-    w_arrive(0, 2)
     t_oth("t", 2)
     t_nbr("t", 1)
+    t_nbr("t", 3)
+    w_arrive(0, 2)
     w_arrive(1, 2)
-    t_nbr("t", 3)
     t_own("t", 2)
+    w_arrive(2, 1)
     y_own("c", 1, 3)
-    w_arrive(0, 3)
     self_nbr("c")
     t_nbr("t", 2)
-    w_arrive(1, 3)
-    swap_wait()
-    w_start(2)
-    w_share(2)
     y_oth("c", 1, 3, 2)
     self_par("c")
-    w_arrive(0, 4)
-    w_arrive(1, 4)
     t_own("c", 1)
     t_own("c", 3)
     t_oth("c", 1)
     t_oth("c", 3)
     y_own("c", 2)
     t_nbr("c", 0)
+    w_arrive(0, 3)
+    w_arrive(1, 3)
+    w_arrive(2, 2)
+    t_oth("c", 2)
+    t_own("c", 2)
+    t_nbr("c", 1)
+    t_nbr("c", 3)
     gather_rows("t")
-    w_arrive(2, 1)
-    t_oth("c", 2)
+    w_arrive(0, 4)
+    w_arrive(1, 4)
+    w_arrive(2, 3)
+    t_nbr("c", 2)
     w_ready(0)
     w_ready(1)
     project_t()
     activate()
-    t_own("c", 2)
-    t_nbr("c", 1)
-    t_nbr("c", 3)
-    w_arrive(2, 2)
-    t_nbr("c", 2)
-    turn(x_t, x_buf, 0, nz)
-    w_arrive(2, 3)
-    turn(x_t, x_buf, nz, 2 * nz)
+    turn(x_t, x_buf, 0, 2 * nz)
     w_arrive(2, 4)
     w_ready(2)
     gather_rows("c")
@@ -762,14 +761,14 @@
     moe_out, tok_out, gate_out, up_out, down_out,
     moe, res, sel, gate, up, down, tok, lsem, rsem, ssem,
 ):
-    count = res.shape[-1] // BLK
-    width = 2 * BLK
+    count, wide = PARTS, res.shape[-1] // PARTS
+    width = 2 * wide
     loads, moves = [], []
     choose = pltpu.make_async_copy(sel_in, sel, lsem.at[4])
     choose.start()
     parts = []
     for j in range(count):
-        at = pl.ds(j * BLK, BLK)
+        at = pl.ds(j * wide, wide)
         parts.append(pltpu.make_async_copy(res_in.at[:, :, at], res.at[:, :, at], rsem.at[j]))
         parts[-1].start()
     whole = ((moe_in, moe, moe_out), (gate_in, gate, gate_out), (up_in, up, up_out), (down_in, down, down_out))
@@ -780,16 +779,17 @@
     choose.wait()
     for j in range(count):
         parts[j].wait()
-        rows_back = res[:, :, pl.ds(j * BLK, BLK)].reshape(8 * SLAB, BLK)
-        for h in range(2):
-            value = jnp.dot(sel[h], rows_back, preferred_element_type=F32)
-            tok[:, pl.ds((2 * j + h) * BLK, BLK)] = value.astype(BF)
+        for i in range(j * wide // BLK, (j + 1) * wide // BLK):
+            rows_back = res[:, :, pl.ds(i * BLK, BLK)].reshape(8 * SLAB, BLK)
+            for h in range(2):
+                value = jnp.dot(sel[h], rows_back, preferred_element_type=F32)
+                tok[:, pl.ds((2 * i + h) * BLK, BLK)] = value.astype(BF)
         at = pl.ds(j * width, width)
         moves.append(pltpu.make_async_copy(tok.at[:, at], tok_out.at[:, at], ssem.at[4 + j]))
         moves[-1].start()
-        if j < 4:
-            loads[j].wait()
-            moves[j].start()
+        for i in range(j * 4 // PARTS, (j + 1) * 4 // PARTS):
+            loads[i].wait()
+            moves[i].start()
     for move in moves:
         move.wait()
 

time: 145 us -> 140 us (0.966)
  Pallas kernels: 142 us -> 137 us
    pallas_call x1, Pallas kernels: 138 us -> 133 us  [on_device(): pl.pallas_call(kernel, out_shape=(shapes[0], back, chosen) + shapes[2:],...]
where the time goes in v4:
time: 140 us; the launch traced here: 137 us
  Pallas kernels  137 us (98%)
    pallas_call x1, Pallas kernels, on_device(): pl.pallas_call(kernel, out_shape=(shapes[0], back, chosen) + shapes[2:],...  133 us
    pallas_call x1, Pallas kernels, on_device(): pl.pallas_call(finish, out_shape=shapes, in_specs=[hbm] * 6, out_specs=(h...  3.53 us

profile of v4, /device:TPU:14, one launch (start us, length us, event | category | flops | bytes accessed | tf_op | source)
XLA Modules:
  0.0 137.4 jit_solution(9913941403631161069)
XLA Ops:
  0.6 133.3 %shard_map.110 = (bf16[128,4096]{1,0:T(8,128)(2,1)}, bf16[8,48,2048]{2,1,0:T(8,128)(2,1)}, bf16[2,128,384]{2,1,0:T(8,128)(2,1)}, f32[256,384]{1,0:T(8,128)}, f32[256,384]{1,0:T(8,128)}, /*index=5*/f32[256,384]{1,0:T(8,128)}) custom-call(bf16[128,4096]{1,0:T(8,128)(2,1)} %tok_hbm.1, s32[1,128]{1,0:T(1,128)} %bitcast.2, f32[1,128]{1,0:T(1,128)} %bitcast.3, ...), custom_call_target="tpu_custom_call" | custom-call | flops 10871635968 | bytes 4194304 | tf_op jit(solution)/shard_map/pallas_call | solution.py:816
  133.9 3.5 %shard_map.111 = (bf16[128,4096]{1,0:T(8,128)(2,1)}, bf16[128,4096]{1,0:T(8,128)(2,1)}, f32[256,384]{1,0:T(8,128)}, f32[256,384]{1,0:T(8,128)}, f32[256,384]{1,0:T(8,128)}) custom-call(bf16[128,4096]{1,0:T(8,128)(2,1)} %get-tuple-element.11.moe_in, bf16[8,48,2048]{2,1,0:T(8,128)(2,1)} %get-tuple-element.12.res_in, ...), custom_call_target="tpu_custom_call" | custom-call | tf_op jit(solution)/shard_map/pallas_call | solution.py:881

commit v5 on v4

--- a/solution.py
+++ b/solution.py
@@ -16,7 +16,7 @@
 SLAB = 2 * CAP
 BLK = 256
 PARTS = 4
-N_SEND, N_RECV = 14, 123
+N_SEND, N_RECV = 14, 126
 
 
 def kernel(
@@ -91,7 +91,7 @@
 
     def recv_group(key):
         if key[0] in ("par", "fwd"):
-            return ("pair", key[1])
+            return key[:2]
         return key[:2] if key[0] == "ws" else key
 
     def numbered(slots, name):
@@ -280,11 +280,13 @@
 
     wide = 512
 
-    def gather_rows(ph):
+    def gather_rows(ph, groups=(OWN, PAR, NBR, FWD)):
         s, own, oth, par, nbr, fwd = stores[ph]
         for r in range(4):
-            got("par", ph, r)
-            got("fwd", ph, r)
+            if PAR in groups:
+                got("par", ph, r)
+            if FWD in groups:
+                got("fwd", ph, r)
 
         def slab(g, r, at):
             if g == OWN:
@@ -299,7 +301,7 @@
 
         def body(j, carry):
             at = pl.ds(pl.multiple_of(j * wide, wide), wide)
-            for g in range(4):
+            for g in groups:
                 for r in (0, 2):
                     first, second = slab(g, r, at), slab(g, r + 1, at)
                     base = (g * 4 + r) * CAP
@@ -336,19 +338,21 @@
 
         lax.fori_loop(0, nz, body, 0)
 
-    def project_c():
-        pre[:, 2 * units:] = jnp.zeros((rows, 2 * units), F32)
+    def project_c(part_of):
+        count = rows // 2
+        here = slice(part_of * count, (part_of + 1) * count)
+        pre[here, 2 * units:] = jnp.zeros((count, 2 * units), F32)
 
         def body(j, carry):
             for k in range(2):
                 acc = None
                 for i in range(2):
                     term = jnp.dot(
-                        g_buf[:, block(2 * j + i)], w_all[k, 2 * j + i, :, cols(2)],
+                        g_buf[here, block(2 * j + i)], w_all[k, 2 * j + i, :, cols(2)],
                         preferred_element_type=F32,
                     )
                     acc = term if acc is None else acc + term
-                pre[:, cols(2 + k)] += acc
+                pre[here, cols(2 + k)] += acc
             return carry
 
         lax.fori_loop(0, nz // 2, body, 0)
@@ -358,13 +362,13 @@
             return pre[at, cols(2)] * low + pre[at, cols(3)] * (1.0 - low)
 
         def split(i, carry):
-            at = pl.ds(pl.multiple_of(i * tall, tall), tall)
+            at = pl.ds(pl.multiple_of(part_of * count + i * tall, tall), tall)
             gh_out[at, :] = pick(at, 1 - hh).astype(BF)
             pre[at, cols(2)] = pick(at, hh)
             return carry
 
-        lax.fori_loop(0, rows // tall, split, 0)
-        send(("gh",), gh_out, gh_in, partner)
+        lax.fori_loop(0, count // tall, split, 0)
+        send(("gh", part_of), gh_out.at[here], gh_in.at[here], partner)
 
     tall = 32
 
@@ -385,8 +389,9 @@
             hid[1 - hh, g * group:(g + 1) * group, :] = hid_in[m * group:(m + 1) * group, :]
 
     def differentiate():
-        got("gh")
         for g in range(4):
+            got("gh", g // 2)
+
             def body(i, carry, g=g):
                 at = pl.ds(pl.multiple_of(g * group + i * tall, tall), tall)
                 there = pl.ds(pl.multiple_of(MIRROR[g] * group + i * tall, tall), tall)
@@ -688,8 +693,10 @@
     turn(x_t, x_buf, 0, 2 * nz)
     w_arrive(2, 4)
     w_ready(2)
-    gather_rows("c")
-    project_c()
+    gather_rows("c", (OWN, PAR))
+    project_c(0)
+    gather_rows("c", (NBR, FWD))
+    project_c(1)
     drain("w", "ws")
     turn(g_t, g_buf, 0, nz)
     join_hidden()
@@ -697,7 +704,8 @@
     weight_grads("d", 1 - c, True)
     weight_grads("d", c, False)
     ring((2, 0))
-    got("gh")
+    got("gh", 0)
+    got("gh", 1)
     feed(5)
     differentiate()
     weight_grads("gu", 1 - c, True)

time: 140 us -> 140 us (level)
  no operation moved by 1% of the time
where the time goes in v5:
time: 140 us; the launch traced here: 137 us
  Pallas kernels  137 us (98%)
    pallas_call x1, Pallas kernels, on_device(): pl.pallas_call(kernel, out_shape=(shapes[0], back, chosen) + shapes[2:],...  133 us
    pallas_call x1, Pallas kernels, on_device(): pl.pallas_call(finish, out_shape=shapes, in_specs=[hbm] * 6, out_specs=(h...  3.53 us

profile of v5, /device:TPU:14, one launch (start us, length us, event | category | flops | bytes accessed | tf_op | source)
XLA Modules:
  0.0 137.5 jit_solution(1571759837736567615)
XLA Ops:
  0.6 133.3 %shard_map.110 = (bf16[128,4096]{1,0:T(8,128)(2,1)}, bf16[8,48,2048]{2,1,0:T(8,128)(2,1)}, bf16[2,128,384]{2,1,0:T(8,128)(2,1)}, f32[256,384]{1,0:T(8,128)}, f32[256,384]{1,0:T(8,128)}, /*index=5*/f32[256,384]{1,0:T(8,128)}) custom-call(bf16[128,4096]{1,0:T(8,128)(2,1)} %tok_hbm.1, s32[1,128]{1,0:T(1,128)} %bitcast.2, f32[1,128]{1,0:T(1,128)} %bitcast.3, ...), custom_call_target="tpu_custom_call" | custom-call | flops 10871635968 | bytes 4194304 | tf_op jit(solution)/shard_map/pallas_call | solution.py:824
  133.9 3.5 %shard_map.111 = (bf16[128,4096]{1,0:T(8,128)(2,1)}, bf16[128,4096]{1,0:T(8,128)(2,1)}, f32[256,384]{1,0:T(8,128)}, f32[256,384]{1,0:T(8,128)}, f32[256,384]{1,0:T(8,128)}) custom-call(bf16[128,4096]{1,0:T(8,128)(2,1)} %get-tuple-element.11.moe_in, bf16[8,48,2048]{2,1,0:T(8,128)(2,1)} %get-tuple-element.12.res_in, ...), custom_call_target="tpu_custom_call" | custom-call | tf_op jit(solution)/shard_map/pallas_call | solution.py:889

commit v6 on v5

--- a/solution.py
+++ b/solution.py
@@ -787,6 +787,9 @@
     choose.wait()
     for j in range(count):
         parts[j].wait()
+        for i in range(j * 4 // PARTS, (j + 1) * 4 // PARTS):
+            loads[i].wait()
+            moves[i].start()
         for i in range(j * wide // BLK, (j + 1) * wide // BLK):
             rows_back = res[:, :, pl.ds(i * BLK, BLK)].reshape(8 * SLAB, BLK)
             for h in range(2):
@@ -795,9 +798,6 @@
         at = pl.ds(j * width, width)
         moves.append(pltpu.make_async_copy(tok.at[:, at], tok_out.at[:, at], ssem.at[4 + j]))
         moves[-1].start()
-        for i in range(j * 4 // PARTS, (j + 1) * 4 // PARTS):
-            loads[i].wait()
-            moves[i].start()
     for move in moves:
         move.wait()
 

time: 140 us -> 140 us (level)
  no operation moved by 1% of the time
where the time goes in v6:
time: 140 us; the launch traced here: 138 us
  Pallas kernels  137 us (98%)
    pallas_call x1, Pallas kernels, on_device(): pl.pallas_call(kernel, out_shape=(shapes[0], back, chosen) + shapes[2:],...  133 us
    pallas_call x1, Pallas kernels, on_device(): pl.pallas_call(finish, out_shape=shapes, in_specs=[hbm] * 6, out_specs=(h...  3.63 us

profile of v6, /device:TPU:14, one launch (start us, length us, event | category | flops | bytes accessed | tf_op | source)
XLA Modules:
  0.0 137.6 jit_solution(2516232517916711627)
XLA Ops:
  0.6 133.3 %shard_map.110 = (bf16[128,4096]{1,0:T(8,128)(2,1)}, bf16[8,48,2048]{2,1,0:T(8,128)(2,1)}, bf16[2,128,384]{2,1,0:T(8,128)(2,1)}, f32[256,384]{1,0:T(8,128)}, f32[256,384]{1,0:T(8,128)}, /*index=5*/f32[256,384]{1,0:T(8,128)}) custom-call(bf16[128,4096]{1,0:T(8,128)(2,1)} %tok_hbm.1, s32[1,128]{1,0:T(1,128)} %bitcast.2, f32[1,128]{1,0:T(1,128)} %bitcast.3, ...), custom_call_target="tpu_custom_call" | custom-call | flops 10871635968 | bytes 4194304 | tf_op jit(solution)/shard_map/pallas_call | solution.py:824
  133.9 3.6 %shard_map.111 = (bf16[128,4096]{1,0:T(8,128)(2,1)}, bf16[128,4096]{1,0:T(8,128)(2,1)}, f32[256,384]{1,0:T(8,128)}, f32[256,384]{1,0:T(8,128)}, f32[256,384]{1,0:T(8,128)}) custom-call(bf16[128,4096]{1,0:T(8,128)(2,1)} %get-tuple-element.11.moe_in, bf16[8,48,2048]{2,1,0:T(8,128)(2,1)} %get-tuple-element.12.res_in, ...), custom_call_target="tpu_custom_call" | custom-call | tf_op jit(solution)/shard_map/pallas_call | solution.py:889
